TPU v7x, 128 devices: a whole 4x4x4 slice. The times are simulated.
128 devices in a mesh: node: 16 (over x, z), tensor: 8 (over y, core).
Axes of the slice: x: 4, y: 4, z: 4, core: 2. Of those that a mesh axis runs over, the one named last changes fastest.
Arguments:
- tokens: bfloat16 [4096, 3584], P(('node', 'tensor')), may hold values from -24 to 24
- out_grad: bfloat16 [4096, 3584], P(('node', 'tensor')), may hold values from -24 to 24
- gate_weights: bfloat16 [4096, 2], P(('node', 'tensor')), may hold values from 0.099609375 to 1
- expert_ids: int32 [4096, 2], P(('node', 'tensor')), may hold values from 0 to 15, as said below
- dense_gate: bfloat16 [3584, 3072], P(None, 'tensor'), may hold values from -0.09375 to 0.09375
- dense_up: bfloat16 [3584, 3072], P(None, 'tensor'), may hold values from -0.09375 to 0.09375
- dense_down: bfloat16 [3584, 3072], P(None, 'tensor'), may hold values from -0.109375 to 0.109375
- expert_gate: bfloat16 [16, 3584, 3072], P('node', None, 'tensor'), may hold values from -0.09375 to 0.09375
- expert_up: bfloat16 [16, 3584, 3072], P('node', None, 'tensor'), may hold values from -0.09375 to 0.09375
- expert_down: bfloat16 [16, 3584, 3072], P('node', None, 'tensor'), may hold values from -0.109375 to 0.109375
Outputs:
- input_grad: bfloat16 [4096, 3584], P(('node', 'tensor'))
- gate_weight_grad: float32 [4096, 2], P(('node', 'tensor'))
- dense_gate_grad: bfloat16 [3584, 3072], P('node', 'tensor')
- dense_up_grad: bfloat16 [3584, 3072], P('node', 'tensor')
- dense_down_grad: bfloat16 [3584, 3072], P('node', 'tensor')
- expert_gate_grad: bfloat16 [16, 3584, 3072], P('node', None, 'tensor')
- expert_up_grad: bfloat16 [16, 3584, 3072], P('node', None, 'tensor')
- expert_down_grad: bfloat16 [16, 3584, 3072], P('node', None, 'tensor')
Inputs may be any that keep to these rules, and one draw needn't show every extreme that they name: `expert_ids`: each row names two different experts. In the rows of one device (aligned blocks of 32 rows) no expert is named more than 8 times, and one expert is named exactly 8 times in the rows of every device.
All inputs are finite; a program needn't handle non-finite values.
Results may differ from a plain program's by a relative error of at most 0.02.
Values may be sent and summed in bfloat16 or wider, within the bound.
A program may use at most 192 MiB of HBM per device.

v0:
```python
import jax
import jax.numpy as jnp
from jax import lax
from jax.experimental import pallas as pl
from jax.experimental.pallas import tpu as pltpu
from jax.sharding import PartitionSpec as P

MESH = pl.DeviceIdType.MESH
BF16 = jnp.bfloat16
F32 = jnp.float32
SIDE = 4
CORES = 2
ANY = pl.BlockSpec(memory_space=pl.ANY)
VMEM = pl.BlockSpec(memory_space=pltpu.VMEM)


def place():
    node = lax.axis_index("node")
    tensor = lax.axis_index("tensor")
    return (
        lax.div(node, SIDE),
        lax.rem(node, SIDE),
        lax.div(tensor, CORES),
        lax.rem(tensor, CORES),
    )


def turn(position, steps):
    return lax.rem(position + steps, SIDE)


def meet(peers):
    barrier = pltpu.get_barrier_semaphore()
    for peer in peers:
        pl.semaphore_signal(barrier, inc=1, device_id=peer, device_id_type=MESH)
    pl.semaphore_wait(barrier, len(peers))


class Net:
    def __init__(self, send_sems, recv_sems):
        self.send_sems, self.recv_sems = send_sems, recv_sems
        self.copies = []

    def start(self, src, dst, peer):
        index = len(self.copies)
        copy = pltpu.make_async_remote_copy(
            src_ref=src,
            dst_ref=dst,
            send_sem=self.send_sems.at[index],
            recv_sem=self.recv_sems.at[index],
            device_id=peer,
            device_id_type=MESH,
        )
        copy.start()
        self.copies.append(copy)
        return copy

    def drain(self):
        for copy in self.copies:
            copy.wait_send()


def total(dst, sources, scale=None, slab=16):
    rows = dst.shape[-2]
    leads = [()]
    for size in dst.shape[:-2]:
        leads = [lead + (i,) for lead in leads for i in range(size)]
    for lead in leads:

        def body(i, carry, lead=lead):
            at = lead + (pl.ds(pl.multiple_of(i * slab, slab), slab), slice(None))
            value = sources[0][at].astype(F32)
            for source in sources[1:]:
                value = value + source[at].astype(F32)
            if scale is not None:
                value = value * scale
            dst[at] = value.astype(dst.dtype)
            return carry

        lax.fori_loop(0, rows // slab, body, 0)


def node_peers(x, z, tensor):
    peers = []
    for dx in range(SIDE):
        for dz in range(SIDE):
            if dx or dz:
                peers.append((turn(x, dx) * SIDE + turn(z, dz), tensor))
    return peers


class Gather:
    def __init__(self, net, node, y, core, own, whole, rows):
        self.net, self.own, self.whole, self.rows = net, own, whole, rows
        self.me = y * CORES + core
        self.right_at = turn(y, 1) * CORES + core
        self.left_at = turn(y, SIDE - 1) * CORES + core
        self.far_at = turn(y, 2) * CORES + core
        self.right = (node, self.right_at)
        self.left = (node, self.left_at)
        self.partner = (node, y * CORES + 1 - core)
        self.crossed = {}

    def chunk(self, half, at):
        return self.whole[half].at[pl.ds(pl.multiple_of(at * self.rows, self.rows), self.rows)]

    def pass_on(self, half, at, name):
        ref = self.chunk(half, at)
        self.crossed[name, half] = self.net.start(ref, ref, self.partner)

    def start(self):
        send = self.net.start
        me, own = self.me, self.own
        self.to_right, self.to_left = [None] * 2, [None] * 2
        for step in range(2):
            self.to_right[step] = send(own[step], self.chunk(step, me), self.right)
            self.to_left[1 - step] = send(own[1 - step], self.chunk(1 - step, me), self.left)
        for half in range(2):
            self.crossed["own", half] = send(own[half], self.chunk(half, me), self.partner)

    def relay(self):
        send = self.net.start
        left_at, right_at = self.left_at, self.right_at
        self.to_right[0].wait_recv()
        self.relay_right = send(self.chunk(0, left_at), self.chunk(0, left_at), self.right)
        self.pass_on(0, left_at, "left")
        self.to_left[1].wait_recv()
        self.relay_left = send(self.chunk(1, right_at), self.chunk(1, right_at), self.left)
        self.pass_on(1, right_at, "right")

    def relay_rest(self):
        self.to_right[1].wait_recv()
        self.pass_on(1, self.left_at, "left")
        self.to_left[0].wait_recv()
        self.pass_on(0, self.right_at, "right")

    def relay_far(self):
        self.relay_right.wait_recv()
        self.pass_on(0, self.far_at, "far")
        self.relay_left.wait_recv()
        self.pass_on(1, self.far_at, "far")

    def arrive(self, name):
        for half in range(2):
            self.crossed[name, half].wait_recv()


class RingSum:
    def __init__(self, net, position, right, left, part, relayed, from_left, from_right):
        self.net, self.right, self.left, self.part = net, right, left, part
        self.relayed, self.from_left, self.from_right = relayed, from_left, from_right
        self.ahead, self.far, self.behind = (turn(position, k) for k in (1, 2, 3))

    def start_far(self):
        send, part = self.net.start, self.part
        self.relay_right = send(part(self.far, 0), self.relayed(0), self.right)
        self.relay_left = send(part(self.far, 1), self.relayed(1), self.left)

    def start_ahead(self):
        self.direct_right = self.net.start(self.part(self.ahead, 1), self.from_left(1), self.right)

    def start_behind(self):
        self.direct_left = self.net.start(self.part(self.behind, 0), self.from_right(0), self.left)

    def middle(self):
        send, part = self.net.start, self.part
        self.relay_right.wait_recv()
        mine = part(self.ahead, 0)
        total(mine, [mine, self.relayed(0)])
        self.sum_right = send(mine, self.from_left(0), self.right)
        self.relay_left.wait_recv()
        mine = part(self.behind, 1)
        total(mine, [mine, self.relayed(1)])
        self.sum_left = send(mine, self.from_right(1), self.left)

    def finish(self):
        for copy in (self.direct_right, self.direct_left, self.sum_right, self.sum_left):
            copy.wait_recv()


NT = (((1,), (1,)), ((), ()))
TN = (((0,), (0,)), ((), ()))
TILE = 512
FORWARD_COPIES = 2 * 14 + 15 + 24


def silu_parts(pre_gate):
    sigma = jax.nn.sigmoid(pre_gate)
    return (pre_gate * sigma, sigma * (1.0 + pre_gate * (1.0 - sigma)))


def unit_grads(rows_x, rows_dy, w_both, w_down, parts, hidden_out):
    hid = w_down.shape[1]
    pre = jnp.dot(rows_x[...], w_both[...], preferred_element_type=F32)
    hidden_grad = jnp.dot(rows_dy[...], w_down[...], preferred_element_type=F32)
    pre_up = pre[:, hid:]
    activated, derivative = silu_parts(pre[:, :hid])
    hidden = activated * pre_up
    parts[:, pl.ds(0, hid)] = (hidden_grad * pre_up * derivative).astype(BF16)
    parts[:, pl.ds(hid, hid)] = (hidden_grad * activated).astype(BF16)
    hidden_out[...] = hidden.astype(BF16)
    return hidden * hidden_grad


def input_term(parts, w_both, out):
    def body(i, carry):
        cols = pl.ds(pl.multiple_of(i * TILE, TILE), TILE)
        out[:, cols] = lax.dot_general(
            parts[...], w_both[cols], NT, preferred_element_type=F32
        ).astype(BF16)
        return carry

    lax.fori_loop(0, out.shape[1] // TILE, body, 0)


def lane_sums(value):
    high = value.astype(BF16)
    low = (value - high.astype(F32)).astype(BF16)
    ones = jnp.ones((8, value.shape[1]), BF16)
    return lax.dot_general(ones, high, NT, preferred_element_type=F32) + lax.dot_general(
        ones, low, NT, preferred_element_type=F32
    )


class WeightSums:
    def __init__(self, net, x, z, tensor, grads, first_bufs, second_bufs):
        self.net, self.x, self.z, self.grads = net, x, z, grads
        self.half = half = grads.shape[2] // 2
        self.first_bufs, self.second_bufs = first_bufs, second_bufs
        pairs = SIDE // 2

        def at(xx, zz):
            return (xx * SIDE + zz, tensor)

        self.around_x = (at(turn(x, 1), z), at(turn(x, 3), z))
        self.around_z = (at(x, turn(z, 1)), at(x, turn(z, 3)))

        def x_part(position, h):
            return grads.at[position, pl.ds(h * pairs, pairs), pl.ds(0, half)]

        def z_part(position, h):
            return grads.at[pl.ds(h * pairs, pairs), position, pl.ds(half, half)]

        def slot(ref, index):
            return lambda h: ref.at[index, pl.ds(h * pairs, pairs)]

        self.rings = [
            RingSum(net, x, *self.around_x, x_part, *(slot(ref, 0) for ref in first_bufs)),
            RingSum(net, z, *self.around_z, z_part, *(slot(ref, 1) for ref in first_bufs)),
        ]

    def middle(self):
        for ring in self.rings:
            ring.middle()

    def second(self):
        half = self.half
        cut = (0, half // 32 * 16 + 16, half)
        unused, from_left, from_right = self.first_bufs

        def rows_half(h):
            return pl.ds(cut[h], cut[h + 1] - cut[h])

        def summed(index):
            return lambda position, h: from_left.at[index, position, rows_half(h)]

        def slot(ref, index):
            return lambda h: ref.at[index, rows_half(h)]

        later = [
            RingSum(self.net, self.z, *self.around_z, summed(0), *(slot(r, 0) for r in self.second_bufs)),
            RingSum(self.net, self.x, *self.around_x, summed(1), *(slot(r, 1) for r in self.second_bufs)),
        ]
        for ring in self.rings:
            ring.finish()
        for steps in (2, 1, 3, 0):
            for index, ring in enumerate(later):
                other = turn((self.z, self.x)[index], steps)
                if index == 0:
                    mine = self.grads.at[self.x, other, pl.ds(0, half)]
                else:
                    mine = self.grads.at[other, self.z, pl.ds(half, half)]
                left, right = from_left.at[index, other], from_right.at[index, other]
                total(left, [mine, left, right])
                if steps == 2:
                    ring.start_far()
                elif steps == 1:
                    ring.start_ahead()
                elif steps == 3:
                    ring.start_behind()
        self.rings = later

    def finish(self, outs):
        half = self.half
        from_left = self.first_bufs[1]
        unused, from_left2, from_right2 = self.second_bufs
        for index, ring in enumerate(self.rings):
            ring.finish()
            own = from_left.at[index, (self.z, self.x)[index]]
            for block, ref in enumerate(outs):
                cols = pl.ds(block * ref.shape[1], ref.shape[1])
                total(
                    ref.at[pl.ds(index * half, half)],
                    [own.at[:, cols], from_left2.at[index, :, cols], from_right2.at[index, :, cols]],
                    scale=1.0 / (SIDE * SIDE),
                )


def forward_kernel(
    tok, grad, outgoing, dense_gate, dense_up, dense_down, expert_gate, expert_up, expert_down,
    out_x, out_dy, out_parts, out_hidden, out_routed, out_dense, shares, out_gate, out_up, out_down,
    tok_all, grad_all, rows_x, rows_dy, landed, w_both, w_down, dense_parts, dense_hidden,
    dense_term, parts, hidden, term, grads, relayed, from_left, from_right,
    relayed2, from_left2, from_right2, send_sems, recv_sems, local_sems,
):
    x, z, y, core = place()
    node, tensor = x * SIDE + z, y * CORES + core
    net = Net(send_sems, recv_sems)
    peers = node_peers(x, z, tensor)
    local_rows, depth = tok.shape
    hid = w_down.shape[1]
    block = landed.shape[0] // (SIDE * SIDE)
    slots = landed.shape[0] // 2
    started = []

    def fetch(src, dst):
        copy = pltpu.make_async_copy(src, dst, local_sems.at[len(started)])
        copy.start()
        started.append(copy)
        return copy

    dense = Gather(net, node, y, core, (tok, grad), (tok_all, grad_all), local_rows)
    routed = Gather(net, node, y, core, None, (rows_x, rows_dy), slots)
    routed.own = [routed.chunk(h, tensor) for h in range(2)]
    sums = WeightSums(
        net, x, z, tensor, grads, (relayed, from_left, from_right),
        (relayed2, from_left2, from_right2),
    )
    meet(peers + [dense.right, dense.left, dense.partner])

    def rows_of(ref, index):
        return ref.at[pl.ds(pl.multiple_of(index * block, block), block)]

    def fetch_weights(gate, up, down):
        return [
            fetch(gate, w_both.at[:, pl.ds(0, hid)]),
            fetch(up, w_both.at[:, pl.ds(hid, hid)]),
            fetch(down, w_down),
        ]

    dense.start()
    arrivals = [net.start(rows_of(outgoing, peer[0]), rows_of(landed, node), peer) for peer in peers]
    kept = [
        fetch(rows_of(outgoing, node), rows_of(landed, node)),
        fetch(tok, dense.chunk(0, tensor)),
        fetch(grad, dense.chunk(1, tensor)),
    ] + fetch_weights(dense_gate, dense_up, dense_down)
    dense.relay()
    dense.relay_rest()
    for copy in arrivals:
        copy.wait_recv()
    kept[0].wait()
    row = lax.broadcasted_iota(jnp.int32, (2 * slots, 2 * slots), 0)
    col = lax.broadcasted_iota(jnp.int32, (2 * slots, 2 * slots), 1)
    half = block // 2
    second = (row >= slots).astype(jnp.int32)
    within = row - second * slots
    source = lax.div(within, half) * block + lax.rem(within, half) + second * half
    table = (col == source).astype(F32).astype(BF16)

    def part(i, carry):
        cols = pl.ds(pl.multiple_of(i * TILE, TILE), TILE)
        value = jnp.dot(table, landed[:, cols], preferred_element_type=F32).astype(BF16)
        routed.own[0][:, cols] = value[:slots]
        routed.own[1][:, cols] = value[slots:]
        return carry

    lax.fori_loop(0, depth // TILE, part, 0)
    routed.start()

    dense.relay_far()
    for name in ("own", "left", "right", "far"):
        dense.arrive(name)
    for copy in kept[1:]:
        copy.wait()
    unit_grads(tok_all, grad_all, w_both, w_down, dense_parts, dense_hidden)
    input_term(dense_parts, w_both, dense_term)
    leaving = [fetch(dense_term, out_dense)]
    weights = fetch_weights(expert_gate, expert_up, expert_down)
    band = depth // SIDE
    x_ring, z_ring = sums.rings
    for steps in (2, 1, 3, 0):
        other = turn(x, steps)
        cols = pl.ds(pl.multiple_of(other * band, band), band)
        value = lax.dot_general(
            tok_all[:, cols], dense_parts[...], TN, preferred_element_type=F32
        ).astype(BF16)
        grads[other, :, :, pl.ds(0, 2 * hid)] = value.reshape(SIDE, band // SIDE, 2 * hid)
        value = lax.dot_general(
            grad_all[:, cols], dense_hidden[...], TN, preferred_element_type=F32
        ).astype(BF16)
        grads[other, :, :, pl.ds(2 * hid, hid)] = value.reshape(SIDE, band // SIDE, hid)
        if steps == 2:
            x_ring.start_far()
        elif steps == 1:
            x_ring.start_ahead()
        elif steps == 3:
            x_ring.start_behind()
    z_ring.start_far()
    z_ring.start_ahead()
    z_ring.start_behind()
    for copy in weights:
        copy.wait()

    pair = CORES * slots
    held = [None, None]

    def expert_rows(which, at):
        rows = pl.ds(pl.multiple_of(at * pair, pair), pair)
        leaving.append(fetch(rows_x.at[rows], out_x.at[rows]))
        leaving.append(fetch(rows_dy.at[rows], out_dy.at[rows]))
        product = unit_grads(
            rows_x.at[rows], rows_dy.at[rows], w_both, w_down, parts.at[rows], hidden.at[rows]
        )
        shares[at] = lane_sums(product)
        if held[which] is not None:
            held[which].wait()
        input_term(parts.at[rows], w_both, term.at[which])
        held[which] = fetch(term.at[which], out_routed.at[rows])

    routed.arrive("own")
    expert_rows(0, y)
    routed.relay()
    routed.relay_rest()
    sums.middle()
    routed.arrive("left")
    expert_rows(1, turn(y, 3))
    routed.arrive("right")
    sums.second()
    expert_rows(0, turn(y, 1))
    routed.relay_far()
    sums.middle()
    routed.arrive("far")
    expert_rows(1, turn(y, 2))
    sums.finish((out_gate, out_up, out_down))
    leaving += [fetch(parts, out_parts), fetch(hidden, out_hidden)] + held
    for copy in leaving:
        copy.wait()
    net.drain()


def forward(tokens, out_grad, outgoing, dense, expert):
    rows, depth = tokens.shape
    hid = dense[0].shape[1]
    count = SIDE * CORES
    slots = outgoing.shape[0] // 2
    node_rows, slot_rows = count * rows, count * slots
    own = depth // (SIDE * SIDE)
    bands = (2, SIDE, own // 2, 3 * hid)
    shape = jax.ShapeDtypeStruct
    return pl.pallas_call(
        forward_kernel,
        out_shape=[
            shape((slot_rows, depth), BF16),
            shape((slot_rows, depth), BF16),
            shape((slot_rows, 2 * hid), BF16),
            shape((slot_rows, hid), BF16),
            shape((slot_rows, depth), BF16),
            shape((node_rows, depth), BF16),
            shape((SIDE, 8, CORES * slots), F32),
        ]
        + [shape((own, hid), BF16)] * 3,
        in_specs=[ANY] * 9,
        out_specs=[ANY] * 6 + [VMEM] * 4,
        scratch_shapes=[
            pltpu.VMEM((node_rows, depth), BF16),
            pltpu.VMEM((node_rows, depth), BF16),
            pltpu.VMEM((slot_rows, depth), BF16),
            pltpu.VMEM((slot_rows, depth), BF16),
            pltpu.VMEM(outgoing.shape, BF16),
            pltpu.VMEM((depth, 2 * hid), BF16),
            pltpu.VMEM((depth, hid), BF16),
            pltpu.VMEM((node_rows, 2 * hid), BF16),
            pltpu.VMEM((node_rows, hid), BF16),
            pltpu.VMEM((node_rows, depth), BF16),
            pltpu.VMEM((slot_rows, 2 * hid), BF16),
            pltpu.VMEM((slot_rows, hid), BF16),
            pltpu.VMEM((2, CORES * slots, depth), BF16),
            pltpu.VMEM((SIDE, SIDE, own, 3 * hid), BF16),
        ]
        + [pltpu.VMEM(bands, BF16)] * 3
        + [pltpu.VMEM((2,) + bands[2:], BF16)] * 3
        + [
            pltpu.SemaphoreType.DMA((FORWARD_COPIES,)),
            pltpu.SemaphoreType.DMA((FORWARD_COPIES,)),
            pltpu.SemaphoreType.DMA((32,)),
        ],
        compiler_params=pltpu.CompilerParams(
            collective_id=0, has_side_effects=True, vmem_limit_bytes=62 << 20
        ),
        name="forward",
    )(tokens, out_grad, outgoing, *dense, *expert)


RETURN_COPIES = 8 + 6 + 15 + 7 + 15


def return_kernel(
    routed, dense, shares, in_x, in_dy, in_parts, in_hidden,
    back, dense_sum, back_shares, gate_grad, up_grad, down_grad,
    partial, from_core, relayed, from_left, from_right, parted, share_in, share_sum,
    rows_x, rows_dy, parts, hidden, tiles, send_sems, recv_sems, local_sems,
):
    x, z, y, core = place()
    node, tensor = x * SIDE + z, y * CORES + core
    net = Net(send_sems, recv_sems)
    peers = node_peers(x, z, tensor)
    count = SIDE * CORES
    mates = [(node, lax.rem(tensor + k, count)) for k in range(1, count)]
    partner = (node, y * CORES + 1 - core)
    right = (node, turn(y, 1) * CORES + core)
    left = (node, turn(y, 3) * CORES + core)
    slots = routed.shape[0] // count
    tokens = dense.shape[0] // count
    rows = slots + tokens
    meet(peers + mates)

    def routed_chunk(at):
        return routed.at[pl.ds(pl.multiple_of(at * slots, slots), slots)]

    def dense_chunk(at):
        return dense.at[pl.ds(pl.multiple_of(at * tokens, tokens), tokens)]

    order = [turn(y, k) for k in (2, 1, 3, 0)]
    crossed = []
    mine = []
    used = [9]

    def fetch(src, dst):
        copy = pltpu.make_async_copy(src, dst, local_sems.at[used[0]])
        copy.start()
        used[0] += 1
        return copy

    for k, other in enumerate(order):
        theirs = other * CORES + 1 - core
        crossed.append(
            (
                net.start(routed_chunk(theirs), from_core.at[other, pl.ds(0, slots)], partner),
                net.start(dense_chunk(theirs), from_core.at[other, pl.ds(slots, tokens)], partner),
            )
        )
        ours = other * CORES + core
        mine.append(
            (
                pltpu.make_async_copy(
                    routed_chunk(ours), partial.at[other, pl.ds(0, slots)], local_sems.at[2 * k]
                ),
                pltpu.make_async_copy(
                    dense_chunk(ours),
                    partial.at[other, pl.ds(slots, tokens)],
                    local_sems.at[2 * k + 1],
                ),
            )
        )
        for copy in mine[-1]:
            copy.start()
    share_copies = [
        net.start(shares.at[lax.div(mate[1], CORES)], share_in.at[tensor], mate) for mate in mates
    ]
    count_tiles = routed.shape[1] // TILE
    hid = hidden.shape[1]
    loads = [[fetch(in_parts, parts), fetch(in_hidden, hidden)]]
    for i in range(count_tiles):
        cols = pl.ds(i * TILE, TILE)
        loads.append(
            [fetch(in_x.at[:, cols], rows_x.at[:, cols]), fetch(in_dy.at[:, cols], rows_dy.at[:, cols])]
        )
    written = []

    def weight_tiles(first, last):
        for i in range(first, last):
            for copy in (loads[0] if i == 0 else []) + loads[i + 1]:
                copy.wait()
            if i >= 2:
                for copy in written[i - 2]:
                    copy.wait()
            cols, tile = pl.ds(i * TILE, TILE), tiles.at[i % 2]
            tile[:, pl.ds(0, 2 * hid)] = lax.dot_general(
                rows_x[:, cols], parts[...], TN, preferred_element_type=F32
            ).astype(BF16)
            tile[:, pl.ds(2 * hid, hid)] = lax.dot_general(
                rows_dy[:, cols], hidden[...], TN, preferred_element_type=F32
            ).astype(BF16)
            written.append(
                [
                    fetch(tile.at[:, pl.ds(k * hid, hid)], out.at[cols])
                    for k, out in enumerate((gate_grad, up_grad, down_grad))
                ]
            )

    half = rows // 2

    def in_half(ref):
        return lambda h: ref.at[pl.ds(h * half, half)]

    def part(position, h):
        return partial.at[position, pl.ds(h * half, half)]

    ring = RingSum(net, y, right, left, part, in_half(relayed), in_half(from_left), in_half(from_right))
    for k, other in enumerate(order):
        for copy in mine[k]:
            copy.wait()
        for copy in crossed[k]:
            copy.wait_recv()
        total(partial.at[other], [partial.at[other], from_core.at[other]])
        (ring.start_far, ring.start_ahead, ring.start_behind, lambda: None)[k]()
    weight_tiles(0, 1)
    for copy in share_copies:
        copy.wait_recv()
    value = shares[y]
    for k in range(1, count):
        value = value + share_in[lax.rem(tensor + k, count)]
    share_sum[...] = value
    back_shares[node] = value
    share_back = [net.start(share_sum, back_shares.at[node], peer) for peer in peers]
    weight_tiles(1, 4)
    ring.middle()
    weight_tiles(4, 6)
    ring.finish()
    own = partial.at[y]
    total(dense_sum, [r.at[pl.ds(slots, tokens)] for r in (own, from_left, from_right)])
    total(own.at[pl.ds(0, slots)], [r.at[pl.ds(0, slots)] for r in (own, from_left, from_right)])
    block = 2 * slots // (SIDE * SIDE)
    short = block // 2
    row = lax.broadcasted_iota(jnp.int32, (2 * slots, slots), 0)
    col = lax.broadcasted_iota(jnp.int32, (2 * slots, slots), 1)
    place_in = lax.rem(row, block)
    second = (place_in >= short).astype(jnp.int32)
    source = lax.div(row, block) * short + place_in - second * short
    hit = (col == source).astype(jnp.int32)
    tables = [(hit * (1 - second)).astype(F32).astype(BF16), (hit * second).astype(F32).astype(BF16)]
    width = 256
    columns = parted.shape[1]

    def cut(i, carry):
        cols = pl.multiple_of(i * width, width)
        value = jnp.dot(
            tables[0], own[pl.ds(0, slots), pl.ds(cols, width)], preferred_element_type=F32
        )
        value = value + jnp.dot(
            tables[1], own[pl.ds(0, slots), pl.ds(cols + columns, width)], preferred_element_type=F32
        )
        parted[:, pl.ds(cols, width)] = value.astype(BF16)
        return carry

    lax.fori_loop(0, columns // width, cut, 0)

    def rows_of(ref, index):
        return ref.at[pl.ds(pl.multiple_of(index * block, block), block)]

    returned = [net.start(rows_of(parted, peer[0]), rows_of(back, node), peer) for peer in peers]
    keep = pltpu.make_async_copy(rows_of(parted, node), rows_of(back, node), local_sems.at[8])
    keep.start()
    weight_tiles(6, count_tiles)
    keep.wait()
    for copies in written[-2:]:
        for copy in copies:
            copy.wait()
    for copy in share_back + returned:
        copy.wait_recv()
    net.drain()


def return_rows(routed, dense, shares, rows_x, rows_dy, parts, hidden):
    count = SIDE * CORES
    width = routed.shape[1]
    slots = routed.shape[0] // count
    tokens = dense.shape[0] // count
    nodes = SIDE * SIDE
    rows = slots + tokens
    return pl.pallas_call(
        return_kernel,
        out_shape=[
            jax.ShapeDtypeStruct((2 * slots, width // 2), BF16),
            jax.ShapeDtypeStruct((tokens, width), F32),
            jax.ShapeDtypeStruct((nodes,) + shares.shape[1:], F32),
        ]
        + [jax.ShapeDtypeStruct((width, hidden.shape[1]), BF16)] * 3,
        in_specs=[ANY, ANY, VMEM] + [ANY] * 4,
        out_specs=[VMEM] * 3 + [ANY] * 3,
        scratch_shapes=[
            pltpu.VMEM((SIDE, rows, width), BF16),
            pltpu.VMEM((SIDE, rows, width), BF16),
            pltpu.VMEM((rows, width), BF16),
            pltpu.VMEM((rows, width), BF16),
            pltpu.VMEM((rows, width), BF16),
            pltpu.VMEM((2 * slots, width // 2), BF16),
            pltpu.VMEM((count,) + shares.shape[1:], F32),
            pltpu.VMEM(shares.shape[1:], F32),
            pltpu.VMEM(rows_x.shape, BF16),
            pltpu.VMEM(rows_dy.shape, BF16),
            pltpu.VMEM(parts.shape, BF16),
            pltpu.VMEM(hidden.shape, BF16),
            pltpu.VMEM((2, TILE, 3 * hidden.shape[1]), BF16),
            pltpu.SemaphoreType.DMA((RETURN_COPIES,)),
            pltpu.SemaphoreType.DMA((RETURN_COPIES,)),
            pltpu.SemaphoreType.DMA((64,)),
        ],
        compiler_params=pltpu.CompilerParams(
            collective_id=1, has_side_effects=True, vmem_limit_bytes=60 << 20
        ),
        name="return_rows",
    )(routed, dense, shares, rows_x, rows_dy, parts, hidden)


def local(
    tokens, out_grad, gate_weights, expert_ids, dense_gate, dense_up, dense_down,
    expert_gate, expert_up, expert_down,
):
    tok_dev, width = tokens.shape
    nodes = SIDE * SIDE
    capacity = 4 * tok_dev // nodes
    block = 2 * capacity
    flat_ids = expert_ids.reshape(-1)
    pair = jnp.arange(2 * tok_dev, dtype=jnp.int32)
    earlier = (flat_ids[:, None] == flat_ids[None, :]) & (pair[None, :] < pair[:, None])
    slot_index = jnp.sum(earlier.astype(jnp.int32), axis=1)
    position = (flat_ids * block + slot_index).reshape(tok_dev, 2)
    row = jnp.arange(nodes * block, dtype=jnp.int32)[None, :, None]
    first_hit = (row == position[:, None, :]).astype(F32)
    second_hit = (row == position[:, None, :] + capacity).astype(F32)
    first_table = jnp.sum(first_hit, axis=2).astype(BF16)
    second_table = jnp.sum(second_hit, axis=2).astype(BF16)
    weight_table = jnp.sum(second_hit * gate_weights.astype(F32)[:, None, :], axis=2).astype(BF16)
    outgoing = lax.dot_general(
        jnp.concatenate([first_table, weight_table], axis=0),
        jnp.concatenate([tokens, out_grad], axis=0),
        (((0,), (0,)), ((), ())),
        preferred_element_type=F32,
    ).astype(BF16)
    (
        rows_x, rows_dy, parts, hidden, routed_input, dense_input, shares,
        dense_gate_grad, dense_up_grad, dense_down_grad,
    ) = forward(
        tokens, out_grad, outgoing, (dense_gate, dense_up, dense_down),
        (expert_gate[0], expert_up[0], expert_down[0]),
    )
    back, dense_sum, back_shares, gate_grad, up_grad, down_grad = return_rows(
        routed_input, dense_input, shares, rows_x, rows_dy, parts, hidden
    )

    picked = jnp.concatenate(
        [
            jnp.dot(first_table, back, preferred_element_type=F32),
            jnp.dot(second_table, back, preferred_element_type=F32),
        ],
        axis=1,
    )
    input_grad = (out_grad.astype(F32) + dense_sum + picked).astype(BF16)
    node, tensor = lax.axis_index("node"), lax.axis_index("tensor")
    start = lax.rem(tensor, CORES) * (nodes * capacity) + node * capacity
    mine = lax.dynamic_slice(back_shares, (0, 0, start), (nodes, 1, capacity)).reshape(1, 1, nodes, capacity)
    expert = jnp.arange(nodes, dtype=jnp.int32)[None, None, :, None]
    slot = jnp.arange(capacity, dtype=jnp.int32)[None, None, None, :]
    chosen = (expert == expert_ids[:, :, None, None]) & (
        slot == slot_index.reshape(tok_dev, 2)[:, :, None, None]
    )
    weighted = jnp.sum(jnp.where(chosen, mine, 0.0), axis=(2, 3))
    gate_weight_grad = weighted / gate_weights.astype(F32)
    return (
        input_grad,
        gate_weight_grad,
        dense_gate_grad,
        dense_up_grad,
        dense_down_grad,
        gate_grad[None],
        up_grad[None],
        down_grad[None],
    )


def solution(mesh):
    rows = P(("node", "tensor"), None)
    dense = P(None, "tensor")
    expert = P("node", None, "tensor")
    summed = P("node", "tensor")
    return jax.shard_map(
        local,
        mesh=mesh,
        in_specs=(rows,) * 4 + (dense,) * 3 + (expert,) * 3,
        out_specs=(rows, rows) + (summed,) * 3 + (expert,) * 3,
        check_vma=False,
    )
```

profile of v0, /device:TPU:0, one launch (start us, length us, event | category | flops | bytes accessed | tf_op | source)
XLA Modules:
  0.0 196.7 jit_solution(6591504049549992980)
XLA Ops:
  0.6 0.8 copy.40
  1.4 0.1 eq.78
  1.5 0.2 convert_reduce_fusion.2
  1.7 0.1 reduce_sum.48
  1.8 0.1 copy.41
  1.9 0.7 broadcast_add_fusion
  2.6 0.7 convert_element_type.35
  3.2 0.1 convert_reduce_fusion
  3.3 2.9 %convolution_convert_fusion.outgoing = bf16[256,3584]{1,0:T(8,128)(2,1)} fusion(bf16[32,3584]{1,0:T(8,128)(2,1)} %grad.1, bf16[32,3584]{1,0:T(8,128)(2,1)} %tok.1, bf16[32,256]{1,0:T(8,128)(2,1)S(1)} %get-tuple-element.41, bf16[32,256]{1,0:T(8,128)(2,1)S(1)} %get-tuple-element.44), kind=kOutput, calls=%fused_computation | convolution fusion | flops 119341056 | bytes 2326528 | tf_op jit(solution)/shard_map/dot_general | solution.py:736
  6.3 107.6 %forward.1 = (bf16[1024,3584]{1,0:T(8,128)(2,1)}, bf16[1024,3584]{1,0:T(8,128)(2,1)}, bf16[1024,768]{1,0:T(8,128)(2,1)}, bf16[1024,384]{1,0:T(8,128)(2,1)}, bf16...) custom-call(bf16[32,3584]{1,0:T(8,128)(2,1)} %tok.1, ...), custom_call_target="tpu_custom_call" | custom-call | tf_op jit(solution)/shard_map/forward/pallas_call | solution.py:461
  113.9 0.0 copy-start.3
  113.9 67.2 %return_rows.1 = (bf16[256,1792]{1,0:T(8,128)(2,1)}, f32[32,3584]{1,0:T(8,128)}, f32[16,8,256]{2,1,0:T(8,128)}, bf16[3584,384]{1,0:T(8,128)(2,1)}, bf16[3584,384]{1,0:T(8,128)(2,1)}, /*index=5*/bf16[3584,384]{1,0:T(8,128)(2,1)}) custom-call(bf16[1024,3584]{1,0:T(8,128)(2,1)} %get-tuple-element.24.routed, bf16[256,3584]{1,0:T(8,128)(2,1)} %get-tuple-element.25.dense, ...), custom_call_target="tpu_custom_call" | custom-call | tf_op jit(solution)/shard_map/return_rows/pallas_call | solution.py:682
  181.1 0.0 copy-start.7
  181.1 0.0 copy-start.8
  181.1 0.0 copy-start.6
  181.1 0.0 copy-start.5
  181.1 1.6 fusion.12
  182.7 1.5 fusion.11
  184.2 1.8 fusion.3
  186.0 0.9 constant_dynamic-slice_fusion
  186.9 0.1 select_reduce_fusion
  187.0 0.0 copy-done.8
  187.0 0.6 convert_divide_fusion
  187.6 0.7 copy.52
  188.3 0.7 copy.53
  189.0 0.0 copy-done.4
  189.0 0.7 copy.54
  189.6 1.5 copy.55
  191.2 1.2 copy-done.1
  192.4 1.5 copy.56
  193.9 1.2 copy-done
  195.2 1.5 copy.57
  (11 shorter events, 0.0 us)
Async XLA Ops:
  113.9 70.4 %copy-start.3 = (bf16[32,3584]{1,0:T(8,128)(2,1)S(1)}, bf16[32,3584]{1,0:T(8,128)(2,1)}, u32[]{:S(2)}) copy-start(bf16[32,3584]{1,0:T(8,128)(2,1)} %grad.1) | copy-start | bytes 688132
  181.1 5.8 %copy-start.7 = (s32[32,2]{0,1:T(2,128)S(1)}, s32[32,2]{0,1:T(2,128)}, u32[]{:S(2)}) copy-start(s32[32,2]{0,1:T(2,128)} %param.13) | copy-start | bytes 772
  181.1 6.0 %copy-start.8 = (bf16[32,2]{0,1:T(2,128)(2,1)S(1)}, bf16[32,2]{0,1:T(2,128)(2,1)}, u32[]{:S(2)}) copy-start(bf16[32,2]{0,1:T(2,128)(2,1)} %param.12) | copy-start | bytes 388
  181.1 6.5 %copy-start.6 = (bf16[224,384]{1,0:T(8,128)(2,1)S(1)}, bf16[224,384]{1,0:T(8,128)(2,1)}, u32[]{:S(2)}) copy-start(bf16[224,384]{1,0:T(8,128)(2,1)} %get-tuple-element.55) | copy-start | bytes 516100
  181.1 7.2 %copy-start.5 = (bf16[224,384]{1,0:T(8,128)(2,1)S(1)}, bf16[224,384]{1,0:T(8,128)(2,1)}, u32[]{:S(2)}) copy-start(bf16[224,384]{1,0:T(8,128)(2,1)} %get-tuple-element.56) | copy-start | bytes 516100
  181.1 7.8 %copy-start.4 = (bf16[224,384]{1,0:T(8,128)(2,1)S(1)}, bf16[224,384]{1,0:T(8,128)(2,1)}, u32[]{:S(2)}) copy-start(bf16[224,384]{1,0:T(8,128)(2,1)} %get-tuple-element.57) | copy-start | bytes 516100
  181.1 8.5 %copy-start.2 = (bf16[3584,384]{1,0:T(8,128)(2,1)S(1)}, bf16[3584,384]{1,0:T(8,128)(2,1)}, u32[]{:S(2)}) copy-start(bf16[3584,384]{1,0:T(8,128)(2,1)} %get-tuple-element.37) | copy-start | bytes 8257540
  189.6 2.8 %copy-start.1 = (bf16[3584,384]{1,0:T(8,128)(2,1)S(1)}, bf16[3584,384]{1,0:T(8,128)(2,1)}, u32[]{:S(2)}) copy-start(bf16[3584,384]{1,0:T(8,128)(2,1)} %get-tuple-element.38) | copy-start | bytes 8257540
  192.4 2.8 %copy-start = (bf16[3584,384]{1,0:T(8,128)(2,1)S(1)}, bf16[3584,384]{1,0:T(8,128)(2,1)}, u32[]{:S(2)}) copy-start(bf16[3584,384]{1,0:T(8,128)(2,1)} %get-tuple-element.39) | copy-start | bytes 8257540
where the time goes:
time: 197 us
  Pallas kernels  175 us (89%)
  local copies, waits for them, and re-layouts  11.1 us (6%)
  matrix products  6.01 us (3%)
  other arithmetic  4.08 us (2%)
    pallas_call x1, Pallas kernels, forward(): pl.pallas_call(forward_kernel, out_shape=[shape((slot_rows, depth), BF16)...  108 us
    pallas_call x1, Pallas kernels, return_rows(): pl.pallas_call(return_kernel, out_shape=[jax.ShapeDtypeStruct((2 * slots,...  67.2 us
    unnamed x25, local copies, waits for them, and re-layouts  9.88 us

commit v1 on v0

--- a/solution.py
+++ b/solution.py
@@ -99,7 +99,7 @@
         self.right = (node, self.right_at)
         self.left = (node, self.left_at)
         self.partner = (node, y * CORES + 1 - core)
-        self.crossed = {}
+        self.crossed, self.to_right, self.to_left = {}, {}, {}
 
     def chunk(self, half, at):
         return self.whole[half].at[pl.ds(pl.multiple_of(at * self.rows, self.rows), self.rows)]
@@ -108,15 +108,12 @@
         ref = self.chunk(half, at)
         self.crossed[name, half] = self.net.start(ref, ref, self.partner)
 
-    def start(self):
+    def start(self, half):
         send = self.net.start
-        me, own = self.me, self.own
-        self.to_right, self.to_left = [None] * 2, [None] * 2
-        for step in range(2):
-            self.to_right[step] = send(own[step], self.chunk(step, me), self.right)
-            self.to_left[1 - step] = send(own[1 - step], self.chunk(1 - step, me), self.left)
-        for half in range(2):
-            self.crossed["own", half] = send(own[half], self.chunk(half, me), self.partner)
+        mine, own = self.chunk(half, self.me), self.own[half]
+        self.to_right[half] = send(own, mine, self.right)
+        self.to_left[half] = send(own, mine, self.left)
+        self.crossed["own", half] = send(own, mine, self.partner)
 
     def relay(self):
         send = self.net.start
@@ -181,7 +178,8 @@
 NT = (((1,), (1,)), ((), ()))
 TN = (((0,), (0,)), ((), ()))
 TILE = 512
-FORWARD_COPIES = 2 * 14 + 15 + 24
+HALF_TILE = 256
+FORWARD_COPIES = 2 * 14 + 2 * 15 + 24
 
 
 def silu_parts(pre_gate):
@@ -307,9 +305,10 @@
 
 
 def forward_kernel(
-    tok, grad, outgoing, dense_gate, dense_up, dense_down, expert_gate, expert_up, expert_down,
+    tok, grad, first_table, second_table, first_weight, second_weight,
+    dense_gate, dense_up, dense_down, expert_gate, expert_up, expert_down,
     out_x, out_dy, out_parts, out_hidden, out_routed, out_dense, shares, out_gate, out_up, out_down,
-    tok_all, grad_all, rows_x, rows_dy, landed, w_both, w_down, dense_parts, dense_hidden,
+    tok_all, grad_all, rows_x, rows_dy, outgoing, landed, w_both, w_down, dense_parts, dense_hidden,
     dense_term, parts, hidden, term, grads, relayed, from_left, from_right,
     relayed2, from_left2, from_right2, send_sems, recv_sems, local_sems,
 ):
@@ -319,8 +318,9 @@
     peers = node_peers(x, z, tensor)
     local_rows, depth = tok.shape
     hid = w_down.shape[1]
-    block = landed.shape[0] // (SIDE * SIDE)
-    slots = landed.shape[0] // 2
+    columns = landed.shape[2]
+    block = landed.shape[1] // (SIDE * SIDE)
+    slots = landed.shape[1] // 2
     started = []
 
     def fetch(src, dst):
@@ -348,40 +348,59 @@
             fetch(down, w_down),
         ]
 
-    dense.start()
-    arrivals = [net.start(rows_of(outgoing, peer[0]), rows_of(landed, node), peer) for peer in peers]
+    dense.start(0)
+    dense.start(1)
+    exchanged = []
+    for h, (source, left, right) in enumerate(
+        ((tok, first_table, second_table), (grad, first_weight, second_weight))
+    ):
+        out, into = outgoing.at[h], landed.at[h]
+        for first in range(0, columns, 2 * HALF_TILE):
+            width = min(2 * HALF_TILE, columns - first)
+            value = lax.dot_general(
+                left[...], source[:, pl.ds(first, width)], TN, preferred_element_type=F32
+            ) + lax.dot_general(
+                right[...], source[:, pl.ds(columns + first, width)], TN, preferred_element_type=F32
+            )
+            out[:, pl.ds(first, width)] = value.astype(BF16)
+        exchanged.append(
+            [net.start(rows_of(out, peer[0]), rows_of(into, node), peer) for peer in peers]
+            + [fetch(rows_of(out, node), rows_of(into, node))]
+        )
     kept = [
-        fetch(rows_of(outgoing, node), rows_of(landed, node)),
         fetch(tok, dense.chunk(0, tensor)),
         fetch(grad, dense.chunk(1, tensor)),
     ] + fetch_weights(dense_gate, dense_up, dense_down)
+    row = lax.broadcasted_iota(jnp.int32, (slots, 2 * slots), 0)
+    col = lax.broadcasted_iota(jnp.int32, (slots, 2 * slots), 1)
+    half = block // 2
+    origin = lax.div(row, half) * block + lax.rem(row, half)
+    tables = [(col == origin + k * half).astype(F32).astype(BF16) for k in range(2)]
+
+    def join(h):
+        for copy in exchanged[h][:-1]:
+            copy.wait_recv()
+        exchanged[h][-1].wait()
+        own, into = routed.own[h], landed.at[h]
+        for first in range(0, columns, 2 * HALF_TILE):
+            width = min(2 * HALF_TILE, columns - first)
+            cols = pl.ds(first, width)
+            for k in range(2):
+                own[:, pl.ds(k * columns + first, width)] = jnp.dot(
+                    tables[k], into[:, cols], preferred_element_type=F32
+                ).astype(BF16)
+
     dense.relay()
     dense.relay_rest()
-    for copy in arrivals:
-        copy.wait_recv()
-    kept[0].wait()
-    row = lax.broadcasted_iota(jnp.int32, (2 * slots, 2 * slots), 0)
-    col = lax.broadcasted_iota(jnp.int32, (2 * slots, 2 * slots), 1)
-    half = block // 2
-    second = (row >= slots).astype(jnp.int32)
-    within = row - second * slots
-    source = lax.div(within, half) * block + lax.rem(within, half) + second * half
-    table = (col == source).astype(F32).astype(BF16)
-
-    def part(i, carry):
-        cols = pl.ds(pl.multiple_of(i * TILE, TILE), TILE)
-        value = jnp.dot(table, landed[:, cols], preferred_element_type=F32).astype(BF16)
-        routed.own[0][:, cols] = value[:slots]
-        routed.own[1][:, cols] = value[slots:]
-        return carry
-
-    lax.fori_loop(0, depth // TILE, part, 0)
-    routed.start()
-
+    join(0)
+    routed.start(0)
     dense.relay_far()
+    join(1)
+    routed.start(1)
+
     for name in ("own", "left", "right", "far"):
         dense.arrive(name)
-    for copy in kept[1:]:
+    for copy in kept:
         copy.wait()
     unit_grads(tok_all, grad_all, w_both, w_down, dense_parts, dense_hidden)
     input_term(dense_parts, w_both, dense_term)
@@ -449,11 +468,11 @@
     net.drain()
 
 
-def forward(tokens, out_grad, outgoing, dense, expert):
+def forward(tokens, out_grad, tables, dense, expert):
     rows, depth = tokens.shape
     hid = dense[0].shape[1]
     count = SIDE * CORES
-    slots = outgoing.shape[0] // 2
+    slots = tables[0].shape[1] // 2
     node_rows, slot_rows = count * rows, count * slots
     own = depth // (SIDE * SIDE)
     bands = (2, SIDE, own // 2, 3 * hid)
@@ -470,14 +489,15 @@
             shape((SIDE, 8, CORES * slots), F32),
         ]
         + [shape((own, hid), BF16)] * 3,
-        in_specs=[ANY] * 9,
+        in_specs=[VMEM] * 6 + [ANY] * 6,
         out_specs=[ANY] * 6 + [VMEM] * 4,
         scratch_shapes=[
             pltpu.VMEM((node_rows, depth), BF16),
             pltpu.VMEM((node_rows, depth), BF16),
             pltpu.VMEM((slot_rows, depth), BF16),
             pltpu.VMEM((slot_rows, depth), BF16),
-            pltpu.VMEM(outgoing.shape, BF16),
+            pltpu.VMEM((2, 2 * slots, depth // 2), BF16),
+            pltpu.VMEM((2, 2 * slots, depth // 2), BF16),
             pltpu.VMEM((depth, 2 * hid), BF16),
             pltpu.VMEM((depth, hid), BF16),
             pltpu.VMEM((node_rows, 2 * hid), BF16),
@@ -499,7 +519,7 @@
             collective_id=0, has_side_effects=True, vmem_limit_bytes=62 << 20
         ),
         name="forward",
-    )(tokens, out_grad, outgoing, *dense, *expert)
+    )(tokens, out_grad, *tables, *dense, *expert)
 
 
 RETURN_COPIES = 8 + 6 + 15 + 7 + 15
@@ -714,6 +734,42 @@
     )(routed, dense, shares, rows_x, rows_dy, parts, hidden)
 
 
+def finish_kernel(out_grad, dense_sum, back, first_table, second_table, *rest):
+    sources, input_grad, results, sems = rest[:6], rest[6], rest[7:13], rest[13]
+    copies = []
+    for source, result in zip(sources, results):
+        pieces = 1 if source.shape[0] < 1024 else 7
+        rows = source.shape[0] // pieces
+        for i in range(pieces):
+            at = pl.ds(i * rows, rows)
+            copies.append(
+                pltpu.make_async_copy(source.at[at], result.at[at], sems.at[len(copies)])
+            )
+            copies[-1].start()
+    columns = back.shape[1]
+    for k, table in enumerate((first_table, second_table)):
+        cols = pl.ds(k * columns, columns)
+        picked = jnp.dot(table[...], back[...], preferred_element_type=F32)
+        input_grad[:, cols] = (
+            out_grad[:, cols].astype(F32) + dense_sum[:, cols] + picked
+        ).astype(BF16)
+    for copy in copies:
+        copy.wait()
+
+
+def finish(out_grad, dense_sum, back, first_table, second_table, grads):
+    return pl.pallas_call(
+        finish_kernel,
+        out_shape=[jax.ShapeDtypeStruct(out_grad.shape, BF16)]
+        + [jax.ShapeDtypeStruct(grad.shape, BF16) for grad in grads],
+        in_specs=[VMEM] * 5 + [ANY] * 6,
+        out_specs=[VMEM] + [ANY] * 6,
+        scratch_shapes=[pltpu.SemaphoreType.DMA((24,))],
+        compiler_params=pltpu.CompilerParams(vmem_limit_bytes=24 << 20),
+        name="finish",
+    )(out_grad, dense_sum, back, first_table, second_table, *grads)
+
+
 def local(
     tokens, out_grad, gate_weights, expert_ids, dense_gate, dense_up, dense_down,
     expert_gate, expert_up, expert_down,
@@ -732,32 +788,25 @@
     second_hit = (row == position[:, None, :] + capacity).astype(F32)
     first_table = jnp.sum(first_hit, axis=2).astype(BF16)
     second_table = jnp.sum(second_hit, axis=2).astype(BF16)
-    weight_table = jnp.sum(second_hit * gate_weights.astype(F32)[:, None, :], axis=2).astype(BF16)
-    outgoing = lax.dot_general(
-        jnp.concatenate([first_table, weight_table], axis=0),
-        jnp.concatenate([tokens, out_grad], axis=0),
-        (((0,), (0,)), ((), ())),
-        preferred_element_type=F32,
-    ).astype(BF16)
+    weights = gate_weights.astype(F32)[:, None, :]
+    first_weight = jnp.sum(first_hit * weights, axis=2).astype(BF16)
+    second_weight = jnp.sum(second_hit * weights, axis=2).astype(BF16)
     (
         rows_x, rows_dy, parts, hidden, routed_input, dense_input, shares,
         dense_gate_grad, dense_up_grad, dense_down_grad,
     ) = forward(
-        tokens, out_grad, outgoing, (dense_gate, dense_up, dense_down),
+        tokens, out_grad, (first_table, second_table, first_weight, second_weight),
+        (dense_gate, dense_up, dense_down),
         (expert_gate[0], expert_up[0], expert_down[0]),
     )
     back, dense_sum, back_shares, gate_grad, up_grad, down_grad = return_rows(
         routed_input, dense_input, shares, rows_x, rows_dy, parts, hidden
     )
 
-    picked = jnp.concatenate(
-        [
-            jnp.dot(first_table, back, preferred_element_type=F32),
-            jnp.dot(second_table, back, preferred_element_type=F32),
-        ],
-        axis=1,
+    input_grad, *weight_grads = finish(
+        out_grad, dense_sum, back, first_table, second_table,
+        (dense_gate_grad, dense_up_grad, dense_down_grad, gate_grad, up_grad, down_grad),
     )
-    input_grad = (out_grad.astype(F32) + dense_sum + picked).astype(BF16)
     node, tensor = lax.axis_index("node"), lax.axis_index("tensor")
     start = lax.rem(tensor, CORES) * (nodes * capacity) + node * capacity
     mine = lax.dynamic_slice(back_shares, (0, 0, start), (nodes, 1, capacity)).reshape(1, 1, nodes, capacity)
@@ -771,12 +820,8 @@
     return (
         input_grad,
         gate_weight_grad,
-        dense_gate_grad,
-        dense_up_grad,
-        dense_down_grad,
-        gate_grad[None],
-        up_grad[None],
-        down_grad[None],
+        *weight_grads[:3],
+        *(value[None] for value in weight_grads[3:]),
     )
 
 

time: 197 us -> 182 us (0.924)
  Pallas kernels: 175 us -> 168 us
  matrix products: 6.01 us -> 0 us
    pallas_call x1, Pallas kernels: 108 us -> 97.4 us  [forward(): pl.pallas_call(forward_kernel, out_shape=[shape((slot_rows, depth), BF16)...]
    dot_general x3 -> x0, matrix products: 6.01 us -> none  [the longest x1 2.94 us: local(): lax.dot_general(jnp.concatenate([first_table, weight_table], axis=0), jnp...]
    pallas_call x0 -> x1, Pallas kernels: none -> 4.58 us  [finish(): pl.pallas_call(finish_kernel, out_shape=[jax.ShapeDtypeStruct(out_grad.sh...]
    unnamed x25 -> x27, local copies, waits for them, and re-layouts: 9.88 us -> 8.32 us
where the time goes in v1:
time: 182 us; the launch traced here: 181 us
  Pallas kernels  168 us (92%)
  local copies, waits for them, and re-layouts  9.53 us (5%)
  other arithmetic  2.93 us (2%)
    pallas_call x1, Pallas kernels, forward(): pl.pallas_call(forward_kernel, out_shape=[shape((slot_rows, depth), BF16)...  97.4 us
    pallas_call x1, Pallas kernels, return_rows(): pl.pallas_call(return_kernel, out_shape=[jax.ShapeDtypeStruct((2 * slots,...  65.9 us
    unnamed x27, local copies, waits for them, and re-layouts  8.32 us
    pallas_call x1, Pallas kernels, finish(): pl.pallas_call(finish_kernel, out_shape=[jax.ShapeDtypeStruct(out_grad.sh...  4.58 us

profile of v1, /device:TPU:0, one launch (start us, length us, event | category | flops | bytes accessed | tf_op | source)
XLA Modules:
  0.0 181.2 jit_solution(8019861311402577024)
XLA Ops:
  0.6 0.8 copy.40
  1.4 0.1 eq.78
  1.5 0.2 convert_reduce_fusion.2
  1.7 0.1 reduce_sum.57
  1.8 0.1 copy.41
  1.9 0.7 broadcast_add_fusion
  2.6 0.7 convert_element_type.30
  3.2 0.7 select_reduce_fusion.1
  3.9 97.4 %forward.1 = (bf16[1024,3584]{1,0:T(8,128)(2,1)}, bf16[1024,3584]{1,0:T(8,128)(2,1)}, bf16[1024,768]{1,0:T(8,128)(2,1)}, bf16[1024,384]{1,0:T(8,128)(2,1)}, bf16...) custom-call(bf16[32,3584]{1,0:T(8,128)(2,1)} %tok.1, ...), custom_call_target="tpu_custom_call" | custom-call | tf_op jit(solution)/shard_map/forward/pallas_call | solution.py:480
  101.4 0.0 copy-start.3
  101.4 0.0 copy-start.6
  101.4 0.0 copy-start.7
  101.4 0.0 copy-start.8
  101.4 0.0 copy-start.9
  101.4 0.0 copy-start.10
  101.4 65.9 %return_rows.1 = (bf16[256,1792]{1,0:T(8,128)(2,1)}, f32[32,3584]{1,0:T(8,128)}, f32[16,8,256]{2,1,0:T(8,128)}, bf16[3584,384]{1,0:T(8,128)(2,1)}, bf16[3584,384]{1,0:T(8,128)(2,1)}, /*index=5*/bf16[3584,384]{1,0:T(8,128)(2,1)}) custom-call(bf16[1024,3584]{1,0:T(8,128)(2,1)} %get-tuple-element.31.routed, bf16[256,3584]{1,0:T(8,128)(2,1)} %get-tuple-element.32.dense, ...), custom_call_target="tpu_custom_call" | custom-call | tf_op jit(solution)/shard_map/return_rows/pallas_call | solution.py:702
  167.3 0.0 copy-done.3
  167.3 0.0 copy-done.6
  167.3 0.0 copy-done.7
  167.3 0.0 copy-done.8
  167.4 0.0 copy-done.9
  167.4 0.0 copy-done.10
  167.4 0.0 copy-start
  167.4 1.8 copy-done
  169.2 1.8 copy-done.1
  170.9 1.8 copy-done.2
  172.7 1.2 copy-done.4
  173.9 1.0 copy-done.5
  174.9 4.6 %finish.1 = (bf16[32,3584]{1,0:T(8,128)(2,1)}, bf16[224,384]{1,0:T(8,128)(2,1)}, bf16[224,384]{1,0:T(8,128)(2,1)}, bf16[224,384]{1,0:T(8,128)(2,1)}, bf16[3584,3...) custom-call(bf16[32,3584]{1,0:T(8,128)(2,1)S(1)} %copy-done.3, f32[32,3584]{1,0:T(8,128)S(1)} %copy-done.5, ...), custom_call_target="tpu_custom_call" | custom-call | tf_op jit(solution)/shard_map/finish/pallas_call | solution.py:761
  179.5 0.9 constant_dynamic-slice_fusion
  180.5 0.1 select_reduce_fusion
  180.6 0.6 convert_divide_fusion
  (10 shorter events, 0.0 us)
Async XLA Ops:
  101.4 66.0 %copy-start.3 = (bf16[32,3584]{1,0:T(8,128)(2,1)S(1)}, bf16[32,3584]{1,0:T(8,128)(2,1)}, u32[]{:S(2)}) copy-start(bf16[32,3584]{1,0:T(8,128)(2,1)} %out_grad.1) | copy-start | bytes 688132
  101.4 66.0 %copy-start.6 = (bf16[224,384]{1,0:T(8,128)(2,1)S(1)}, bf16[224,384]{1,0:T(8,128)(2,1)}, u32[]{:S(2)}) copy-start(bf16[224,384]{1,0:T(8,128)(2,1)} %get-tuple-element.40.rest_0_) | copy-start | bytes 516100
  101.4 66.0 %copy-start.7 = (bf16[224,384]{1,0:T(8,128)(2,1)S(1)}, bf16[224,384]{1,0:T(8,128)(2,1)}, u32[]{:S(2)}) copy-start(bf16[224,384]{1,0:T(8,128)(2,1)} %get-tuple-element.41.rest_1_) | copy-start | bytes 516100
  101.4 66.0 %copy-start.8 = (bf16[224,384]{1,0:T(8,128)(2,1)S(1)}, bf16[224,384]{1,0:T(8,128)(2,1)}, u32[]{:S(2)}) copy-start(bf16[224,384]{1,0:T(8,128)(2,1)} %get-tuple-element.42.rest_2_) | copy-start | bytes 516100
  101.4 66.0 %copy-start.9 = (bf16[32,256]{1,0:T(8,128)(2,1)S(1)}, bf16[32,256]{1,0:T(8,128)(2,1)}, u32[]{:S(2)}) copy-start(bf16[32,256]{1,0:T(8,128)(2,1)} %get-tuple-element.55.second_table) | copy-start | bytes 49156
  101.4 66.0 %copy-start.10 = (bf16[32,256]{1,0:T(8,128)(2,1)S(1)}, bf16[32,256]{1,0:T(8,128)(2,1)}, u32[]{:S(2)}) copy-start(bf16[32,256]{1,0:T(8,128)(2,1)} %get-tuple-element.57.first_table) | copy-start | bytes 49156
  167.4 1.8 copy-start
  169.2 1.8 copy-start.1
  170.9 1.8 copy-start.2
  172.7 1.2 copy-start.4
  173.9 1.0 copy-start.5
  174.9 5.5 %copy-start.11 = (s32[32,2]{0,1:T(2,128)S(1)}, s32[32,2]{0,1:T(2,128)}, u32[]{:S(2)}) copy-start(s32[32,2]{0,1:T(2,128)} %param.13) | copy-start | bytes 772
  174.9 5.7 %copy-start.12 = (bf16[32,2]{0,1:T(2,128)(2,1)S(1)}, bf16[32,2]{0,1:T(2,128)(2,1)}, u32[]{:S(2)}) copy-start(bf16[32,2]{0,1:T(2,128)(2,1)} %param.12) | copy-start | bytes 388

commit v2 on v1

v2 whole, which is shorter than its diff:
```python
import jax
import jax.numpy as jnp
from jax import lax
from jax.experimental import pallas as pl
from jax.experimental.pallas import tpu as pltpu
from jax.sharding import PartitionSpec as P

MESH = pl.DeviceIdType.MESH
BF16 = jnp.bfloat16
F32 = jnp.float32
SIDE = 4
CORES = 2
ANY = pl.BlockSpec(memory_space=pl.ANY)
VMEM = pl.BlockSpec(memory_space=pltpu.VMEM)


def place():
    node = lax.axis_index("node")
    tensor = lax.axis_index("tensor")
    return (
        lax.div(node, SIDE),
        lax.rem(node, SIDE),
        lax.div(tensor, CORES),
        lax.rem(tensor, CORES),
    )


def turn(position, steps):
    return lax.rem(position + steps, SIDE)


def meet(peers):
    barrier = pltpu.get_barrier_semaphore()
    for peer in peers:
        pl.semaphore_signal(barrier, inc=1, device_id=peer, device_id_type=MESH)
    pl.semaphore_wait(barrier, len(peers))


class Net:
    def __init__(self, send_sems, recv_sems):
        self.send_sems, self.recv_sems = send_sems, recv_sems
        self.copies = []
        self.pending = []

    def start(self, src, dst, peer, keep=True):
        index = len(self.copies)
        copy = pltpu.make_async_remote_copy(
            src_ref=src,
            dst_ref=dst,
            send_sem=self.send_sems.at[index],
            recv_sem=self.recv_sems.at[index],
            device_id=peer,
            device_id_type=MESH,
        )
        copy.start()
        self.copies.append(copy)
        if keep:
            self.pending.append(copy)
        return copy

    def drain(self):
        for copy in self.pending:
            copy.wait_send()


def total(dst, sources, scale=None, slab=16):
    rows = dst.shape[-2]
    leads = [()]
    for size in dst.shape[:-2]:
        leads = [lead + (i,) for lead in leads for i in range(size)]
    for lead in leads:

        def body(i, carry, lead=lead):
            at = lead + (pl.ds(pl.multiple_of(i * slab, slab), slab), slice(None))
            value = sources[0][at].astype(F32)
            for source in sources[1:]:
                value = value + source[at].astype(F32)
            if scale is not None:
                value = value * scale
            dst[at] = value.astype(dst.dtype)
            return carry

        lax.fori_loop(0, rows // slab, body, 0)


def node_peers(x, z, tensor):
    peers = []
    for dx in range(SIDE):
        for dz in range(SIDE):
            if dx or dz:
                peers.append((turn(x, dx) * SIDE + turn(z, dz), tensor))
    return peers


class Gather:
    def __init__(self, net, node, y, core, own, whole, rows):
        self.net, self.own, self.whole, self.rows = net, own, whole, rows
        self.me = y * CORES + core
        self.right_at = turn(y, 1) * CORES + core
        self.left_at = turn(y, SIDE - 1) * CORES + core
        self.far_at = turn(y, 2) * CORES + core
        self.right = (node, self.right_at)
        self.left = (node, self.left_at)
        self.partner = (node, y * CORES + 1 - core)
        self.crossed, self.to_right, self.to_left = {}, {}, {}

    def chunk(self, half, at):
        return self.whole[half].at[pl.ds(pl.multiple_of(at * self.rows, self.rows), self.rows)]

    def pass_on(self, half, at, name):
        ref = self.chunk(half, at)
        self.crossed[name, half] = self.net.start(ref, ref, self.partner)

    def start(self, half):
        send = self.net.start
        mine, own = self.chunk(half, self.me), self.own[half]
        self.to_right[half] = send(own, mine, self.right)
        self.to_left[half] = send(own, mine, self.left)
        self.crossed["own", half] = send(own, mine, self.partner)

    def relay(self):
        send = self.net.start
        left_at, right_at = self.left_at, self.right_at
        self.to_right[0].wait_recv()
        self.relay_right = send(self.chunk(0, left_at), self.chunk(0, left_at), self.right)
        self.pass_on(0, left_at, "left")
        self.to_left[1].wait_recv()
        self.relay_left = send(self.chunk(1, right_at), self.chunk(1, right_at), self.left)
        self.pass_on(1, right_at, "right")

    def relay_rest(self):
        self.to_right[1].wait_recv()
        self.pass_on(1, self.left_at, "left")
        self.to_left[0].wait_recv()
        self.pass_on(0, self.right_at, "right")

    def relay_far(self):
        self.relay_right.wait_recv()
        self.pass_on(0, self.far_at, "far")
        self.relay_left.wait_recv()
        self.pass_on(1, self.far_at, "far")

    def arrive(self, name):
        for half in range(2):
            self.crossed[name, half].wait_recv()


class RingSum:
    def __init__(self, net, position, right, left, part, relayed, from_left, from_right):
        self.net, self.right, self.left, self.part = net, right, left, part
        self.relayed, self.from_left, self.from_right = relayed, from_left, from_right
        self.ahead, self.far, self.behind = (turn(position, k) for k in (1, 2, 3))

    def start_far(self):
        send, part = self.net.start, self.part
        self.relay_right = send(part(self.far, 0), self.relayed(0), self.right)
        self.relay_left = send(part(self.far, 1), self.relayed(1), self.left)

    def start_ahead(self):
        self.direct_right = self.net.start(self.part(self.ahead, 1), self.from_left(1), self.right)

    def start_behind(self):
        self.direct_left = self.net.start(self.part(self.behind, 0), self.from_right(0), self.left)

    def middle(self):
        self.absorb()
        self.send_sums()

    def absorb(self):
        self.relay_right.wait_recv()
        mine = self.part(self.ahead, 0)
        total(mine, [mine, self.relayed(0)])
        self.relay_left.wait_recv()
        mine = self.part(self.behind, 1)
        total(mine, [mine, self.relayed(1)])

    def send_sums(self):
        send, part = self.net.start, self.part
        self.sum_right = send(part(self.ahead, 0), self.from_left(0), self.right)
        self.sum_left = send(part(self.behind, 1), self.from_right(1), self.left)

    def finish(self):
        for copy in (self.direct_right, self.direct_left, self.sum_right, self.sum_left):
            copy.wait_recv()


NT = (((1,), (1,)), ((), ()))
TN = (((0,), (0,)), ((), ()))
TILE = 512
HALF_TILE = 256
VMEM_BYTES = 63 << 20
LAYER_COPIES = 2 * 14 + 2 * 15 + 24 + 8 + 12 + 7 + 15 + 2 * 15


def silu_parts(pre_gate):
    sigma = jax.nn.sigmoid(pre_gate)
    return (pre_gate * sigma, sigma * (1.0 + pre_gate * (1.0 - sigma)))


def unit_grads(rows_x, rows_dy, w_both, w_down, parts, hidden_out):
    hid = w_down.shape[1]
    pre = jnp.dot(rows_x[...], w_both[...], preferred_element_type=F32)
    hidden_grad = jnp.dot(rows_dy[...], w_down[...], preferred_element_type=F32)
    pre_up = pre[:, hid:]
    activated, derivative = silu_parts(pre[:, :hid])
    hidden = activated * pre_up
    parts[:, pl.ds(0, hid)] = (hidden_grad * pre_up * derivative).astype(BF16)
    parts[:, pl.ds(hid, hid)] = (hidden_grad * activated).astype(BF16)
    hidden_out[...] = hidden.astype(BF16)
    return hidden * hidden_grad


def input_term(parts, w_both, first, columns, store):
    def body(i, carry):
        at = pl.multiple_of(i * HALF_TILE, HALF_TILE)
        value = lax.dot_general(
            parts[...], w_both[pl.ds(first + at, HALF_TILE)], NT, preferred_element_type=F32
        )
        store(pl.ds(at, HALF_TILE), value.astype(BF16))
        return carry

    lax.fori_loop(0, columns // HALF_TILE, body, 0)


def lane_sums(value):
    high = value.astype(BF16)
    low = (value - high.astype(F32)).astype(BF16)
    ones = jnp.ones((8, value.shape[1]), BF16)
    return lax.dot_general(ones, high, NT, preferred_element_type=F32) + lax.dot_general(
        ones, low, NT, preferred_element_type=F32
    )


class WeightSums:
    def __init__(self, net, x, z, tensor, grads, first_bufs):
        self.net, self.x, self.z, self.grads = net, x, z, grads
        self.half = half = grads.shape[2] // 2
        self.first_bufs = first_bufs
        pairs = SIDE // 2

        def at(xx, zz):
            return (xx * SIDE + zz, tensor)

        self.around_x = (at(turn(x, 1), z), at(turn(x, 3), z))
        self.around_z = (at(x, turn(z, 1)), at(x, turn(z, 3)))

        def x_part(position, h):
            return grads.at[position, pl.ds(h * pairs, pairs), pl.ds(0, half)]

        def z_part(position, h):
            return grads.at[pl.ds(h * pairs, pairs), position, pl.ds(half, half)]

        def slot(ref, index):
            return lambda h: ref.at[index, pl.ds(h * pairs, pairs)]

        self.rings = [
            RingSum(net, x, *self.around_x, x_part, *(slot(ref, 0) for ref in first_bufs)),
            RingSum(net, z, *self.around_z, z_part, *(slot(ref, 1) for ref in first_bufs)),
        ]

    def middle(self):
        for ring in self.rings:
            ring.absorb()
        for ring in self.rings:
            ring.send_sums()

    def second(self):
        half = self.half
        cut = (0, half // 32 * 16 + 16, half)
        relayed, from_left, from_right = self.first_bufs

        def rows_half(h):
            return pl.ds(cut[h], cut[h + 1] - cut[h])

        def summed(index):
            return lambda position, h: from_left.at[index, position, rows_half(h)]

        def slot(index, k):
            return lambda h: relayed.at[index, k, rows_half(h)]

        later = [
            RingSum(self.net, self.z, *self.around_z, summed(0), *(slot(0, k) for k in range(3))),
            RingSum(self.net, self.x, *self.around_x, summed(1), *(slot(1, k) for k in range(3))),
        ]
        for ring in self.rings:
            ring.finish()
        for steps in (2, 1, 3, 0):
            for index, ring in enumerate(later):
                other = turn((self.z, self.x)[index], steps)
                if index == 0:
                    mine = self.grads.at[self.x, other, pl.ds(0, half)]
                else:
                    mine = self.grads.at[other, self.z, pl.ds(half, half)]
                left, right = from_left.at[index, other], from_right.at[index, other]
                total(left, [mine, left, right])
                if steps == 2:
                    ring.start_far()
                elif steps == 1:
                    ring.start_ahead()
                elif steps == 3:
                    ring.start_behind()
        self.rings = later

    def finish(self, outs):
        half = self.half
        relayed, from_left, unused = self.first_bufs
        for index, ring in enumerate(self.rings):
            ring.finish()
            own = from_left.at[index, (self.z, self.x)[index]]
            for block, ref in enumerate(outs):
                cols = pl.ds(block * ref.shape[1], ref.shape[1])
                total(
                    ref.at[pl.ds(index * half, half)],
                    [own.at[:, cols]] + [relayed.at[index, k, :, cols] for k in (1, 2)],
                    scale=1.0 / (SIDE * SIDE),
                )


def layer_kernel(
    tok, grad, first_table, second_table, first_weight, second_weight,
    dense_gate, dense_up, dense_down, expert_gate, expert_up, expert_down,
    back, dense_sum, back_shares, out_gate, out_up, out_down, gate_grad, up_grad, down_grad,
    tok_all, grad_all, rows_x, rows_dy, exchange, w_both, w_down, dense_parts, dense_hidden,
    parts, hidden, grads, relayed, from_left, from_right,
    terms, core_rest, y_relayed, y_left, y_right, shares, share_in, share_sum,
    send_sems, recv_sems, local_sems,
):
    x, z, y, core = place()
    node, tensor = x * SIDE + z, y * CORES + core
    net = Net(send_sems, recv_sems)
    peers = node_peers(x, z, tensor)
    count = SIDE * CORES
    mates = [(node, lax.rem(tensor + k, count)) for k in range(1, count)]
    local_rows, depth = tok.shape
    hid = w_down.shape[1]
    columns = exchange.shape[1]
    stack = exchange.shape[0] // 4
    outgoing = [exchange.at[pl.ds(h * stack, stack)] for h in range(2)]
    landed = [exchange.at[pl.ds((2 + h) * stack, stack)] for h in range(2)]
    block = stack // (SIDE * SIDE)
    slots = stack // 2
    started = []

    def fetch(src, dst):
        copy = pltpu.make_async_copy(src, dst, local_sems.at[len(started)])
        copy.start()
        started.append(copy)
        return copy

    dense = Gather(net, node, y, core, (tok, grad), (tok_all, grad_all), local_rows)
    routed = Gather(net, node, y, core, None, (rows_x, rows_dy), slots)
    routed.own = [routed.chunk(h, tensor) for h in range(2)]
    sums = WeightSums(net, x, z, tensor, grads, (relayed, from_left, from_right))
    meet(peers + mates)

    def rows_of(ref, index):
        return ref.at[pl.ds(pl.multiple_of(index * block, block), block)]

    def fetch_weights(gate, up, down):
        return [
            fetch(gate, w_both.at[:, pl.ds(0, hid)]),
            fetch(up, w_both.at[:, pl.ds(hid, hid)]),
            fetch(down, w_down),
        ]

    dense.start(0)
    dense.start(1)
    exchanged = []
    for h, (source, left, right) in enumerate(
        ((tok, first_table, second_table), (grad, first_weight, second_weight))
    ):
        out, into = outgoing[h], landed[h]
        for first in range(0, columns, 2 * HALF_TILE):
            width = min(2 * HALF_TILE, columns - first)
            value = lax.dot_general(
                left[...], source[:, pl.ds(first, width)], TN, preferred_element_type=F32
            ) + lax.dot_general(
                right[...], source[:, pl.ds(columns + first, width)], TN, preferred_element_type=F32
            )
            out[:, pl.ds(first, width)] = value.astype(BF16)
        exchanged.append(
            [net.start(rows_of(out, peer[0]), rows_of(into, node), peer, False) for peer in peers]
            + [fetch(rows_of(out, node), rows_of(into, node))]
        )
    kept = [
        fetch(tok, dense.chunk(0, tensor)),
        fetch(grad, dense.chunk(1, tensor)),
    ] + fetch_weights(dense_gate, dense_up, dense_down)
    row = lax.broadcasted_iota(jnp.int32, (slots, 2 * slots), 0)
    col = lax.broadcasted_iota(jnp.int32, (slots, 2 * slots), 1)
    half = block // 2
    origin = lax.div(row, half) * block + lax.rem(row, half)
    tables = [(col == origin + k * half).astype(F32).astype(BF16) for k in range(2)]
    row = lax.broadcasted_iota(jnp.int32, (2 * slots, slots), 0)
    col = lax.broadcasted_iota(jnp.int32, (2 * slots, slots), 1)
    origin = lax.div(row, block) * half + lax.rem(row, block)
    back_tables = [
        (jnp.logical_and(col == origin - k * half, lax.div(lax.rem(row, block), half) == k))
        .astype(F32)
        .astype(BF16)
        for k in range(2)
    ]

    def join(h):
        for copy in exchanged[h][:-1]:
            copy.wait()
        exchanged[h][-1].wait()
        own, into = routed.own[h], landed[h]
        for first in range(0, columns, 2 * HALF_TILE):
            width = min(2 * HALF_TILE, columns - first)
            cols = pl.ds(first, width)
            for k in range(2):
                own[:, pl.ds(k * columns + first, width)] = jnp.dot(
                    tables[k], into[:, cols], preferred_element_type=F32
                ).astype(BF16)

    dense.relay()
    dense.relay_rest()
    join(0)
    routed.start(0)
    dense.relay_far()
    join(1)
    routed.start(1)

    for name in ("own", "left", "right", "far"):
        dense.arrive(name)
    for copy in kept:
        copy.wait()
    unit_grads(tok_all, grad_all, w_both, w_down, dense_parts, dense_hidden)

    def side(other_core):
        return lax.rem(core + other_core, CORES)

    for c in range(2):

        def keep_dense(cols, value, c=c):
            for at in range(SIDE):
                for k in range(CORES):
                    first = (at * CORES + k) * local_rows
                    terms[c, side(k), at, pl.ds(slots, local_rows), cols] = value[
                        first : first + local_rows
                    ]

        input_term(dense_parts, w_both, c * columns, columns, keep_dense)
    weights = fetch_weights(expert_gate, expert_up, expert_down)
    band = depth // SIDE
    x_ring, z_ring = sums.rings
    for steps in (2, 1, 3, 0):
        other = turn(x, steps)
        cols = pl.ds(pl.multiple_of(other * band, band), band)
        value = lax.dot_general(
            tok_all[:, cols], dense_parts[...], TN, preferred_element_type=F32
        ).astype(BF16)
        grads[other, :, :, pl.ds(0, 2 * hid)] = value.reshape(SIDE, band // SIDE, 2 * hid)
        value = lax.dot_general(
            grad_all[:, cols], dense_hidden[...], TN, preferred_element_type=F32
        ).astype(BF16)
        grads[other, :, :, pl.ds(2 * hid, hid)] = value.reshape(SIDE, band // SIDE, hid)
        if steps == 2:
            x_ring.start_far()
        elif steps == 1:
            x_ring.start_ahead()
        elif steps == 3:
            x_ring.start_behind()
    z_ring.start_far()
    z_ring.start_ahead()
    z_ring.start_behind()
    for copy in weights:
        copy.wait()

    pair = CORES * slots
    crossed = {}

    def from_core(step, c):
        index, rows = 2 * step + c, slots + local_rows
        fit = exchange.shape[0] // rows
        if index < fit:
            return exchange.at[pl.ds(index * rows, rows)]
        return core_rest.at[index - fit]

    def expert_rows(step, at):
        rows = pl.ds(pl.multiple_of(at * pair, pair), pair)
        product = unit_grads(
            rows_x.at[rows], rows_dy.at[rows], w_both, w_down, parts.at[rows], hidden.at[rows]
        )
        shares[at] = lane_sums(product)
        for c in range(2):

            def keep_routed(cols, value, c=c):
                for k in range(CORES):
                    terms[c, side(k), at, pl.ds(0, slots), cols] = value[k * slots : (k + 1) * slots]

            input_term(parts.at[rows], w_both, c * columns, columns, keep_routed)
            crossed[step, c] = net.start(
                terms.at[c, 1, at], from_core(step, c), routed.partner
            )

    def absorb(step, at, c):
        crossed[step, c].wait_recv()
        mine = terms.at[c, 0, at]
        total(mine, [mine, from_core(step, c)])

    def half_rows(ref, *lead):
        half = ref.shape[-2] // 2
        return lambda h: ref.at[(*lead, pl.ds(h * half, half))]

    y_rings = [
        RingSum(
            net, y, routed.right, routed.left,
            lambda position, h, c=c: half_rows(terms, c, 0, position)(h),
            half_rows(y_relayed, c), half_rows(y_left, c), half_rows(y_right, c),
        )
        for c in range(2)
    ]
    routed.arrive("own")
    expert_rows(0, y)
    routed.relay()
    routed.relay_rest()
    sums.middle()
    routed.arrive("left")
    expert_rows(1, turn(y, 3))
    routed.arrive("right")
    sums.second()
    expert_rows(2, turn(y, 1))
    for c in range(2):
        absorb(1, turn(y, 3), c)
        absorb(2, turn(y, 1), c)
    routed.relay_far()
    for ring in y_rings:
        ring.start_ahead()
        ring.start_behind()
    routed.arrive("far")
    expert_rows(3, turn(y, 2))
    for c in range(2):
        absorb(3, turn(y, 2), c)
        y_rings[c].start_far()
    share_copies = [
        net.start(shares.at[lax.div(mate[1], CORES)], share_in.at[tensor], mate) for mate in mates
    ]
    sums.middle()
    for c in range(2):
        absorb(0, y, c)

    written = []

    def weight_tiles(first, last):
        for i in range(first, last):
            cols = pl.ds(i * TILE, TILE)
            w_both[cols] = lax.dot_general(
                rows_x[:, cols], parts[...], TN, preferred_element_type=F32
            ).astype(BF16)
            w_down[cols] = lax.dot_general(
                rows_dy[:, cols], hidden[...], TN, preferred_element_type=F32
            ).astype(BF16)
            written.append(fetch(w_both.at[cols, pl.ds(0, hid)], gate_grad.at[cols]))
            written.append(fetch(w_both.at[cols, pl.ds(hid, hid)], up_grad.at[cols]))
            written.append(fetch(w_down.at[cols], down_grad.at[cols]))

    weight_tiles(0, 2)
    for copy in share_copies:
        copy.wait_recv()
    value = shares[y]
    for k in range(1, count):
        value = value + share_in[lax.rem(tensor + k, count)]
    share_sum[...] = value
    back_shares[node] = value
    returned = [net.start(share_sum, back_shares.at[node], peer) for peer in peers]
    weight_tiles(2, 3)
    y_rings[0].middle()
    weight_tiles(3, 5)
    y_rings[1].middle()
    sums.finish((out_gate, out_up, out_down))
    count_tiles = depth // TILE
    short = columns // 2
    for c in range(2):
        if c == 0:
            weight_tiles(5, 6)
        y_rings[c].finish()
        own, left, right = terms.at[c, 0, y], y_left.at[c], y_right.at[c]
        landed_rows = [ref.at[pl.ds(0, slots)] for ref in (own, left, right)]
        total(own.at[pl.ds(0, slots)], landed_rows)
        for first in range(0, short, HALF_TILE):
            width = min(HALF_TILE, short - first)
            value = jnp.dot(
                back_tables[0], own[pl.ds(0, slots), pl.ds(first, width)], preferred_element_type=F32
            ) + jnp.dot(
                back_tables[1],
                own[pl.ds(0, slots), pl.ds(short + first, width)],
                preferred_element_type=F32,
            )
            for k in range(2):
                y_relayed[c, pl.ds(0, slots), pl.ds(k * short + first, width)] = value[
                    k * slots : (k + 1) * slots
                ].astype(BF16)

        def parted(index, c=c):
            each = slots // block
            rows = pl.multiple_of(lax.rem(index, each) * block, block)
            cols = pl.multiple_of(lax.div(index, each) * short, 128)
            return y_relayed.at[c, pl.ds(rows, block), pl.ds(cols, short)]

        returned += [net.start(parted(peer[0]), rows_of(back.at[c], node), peer) for peer in peers]
        written.append(fetch(parted(node), rows_of(back.at[c], node)))
        total(
            dense_sum.at[:, pl.ds(c * columns, columns)],
            [ref.at[pl.ds(slots, local_rows)] for ref in (own, left, right)],
        )
    weight_tiles(6, count_tiles)
    for copy in returned:
        copy.wait_recv()
    for copy in written:
        copy.wait()
    net.drain()


def layer(tokens, out_grad, tables, dense, expert):
    rows, depth = tokens.shape
    hid = dense[0].shape[1]
    count = SIDE * CORES
    nodes = SIDE * SIDE
    slots = tables[0].shape[1] // 2
    node_rows, slot_rows = count * rows, count * slots
    own = depth // nodes
    half = depth // 2
    bands = (2, SIDE, own // 2, 3 * hid)
    shape = jax.ShapeDtypeStruct
    share = (8, CORES * slots)
    return pl.pallas_call(
        layer_kernel,
        out_shape=[
            shape((2, 2 * slots, half // 2), BF16),
            shape((rows, depth), F32),
            shape((nodes,) + share, F32),
        ]
        + [shape((own, hid), BF16)] * 3
        + [shape((depth, hid), BF16)] * 3,
        in_specs=[VMEM] * 6 + [ANY] * 6,
        out_specs=[ANY] + [VMEM] * 5 + [ANY] * 3,
        scratch_shapes=[
            pltpu.VMEM((node_rows, depth), BF16),
            pltpu.VMEM((node_rows, depth), BF16),
            pltpu.VMEM((slot_rows, depth), BF16),
            pltpu.VMEM((slot_rows, depth), BF16),
            pltpu.VMEM((8 * slots, half), BF16),
            pltpu.VMEM((depth, 2 * hid), BF16),
            pltpu.VMEM((depth, hid), BF16),
            pltpu.VMEM((node_rows, 2 * hid), BF16),
            pltpu.VMEM((node_rows, hid), BF16),
            pltpu.VMEM((slot_rows, 2 * hid), BF16),
            pltpu.VMEM((slot_rows, hid), BF16),
            pltpu.VMEM((SIDE, SIDE, own, 3 * hid), BF16),
        ]
        + [pltpu.VMEM(bands, BF16)] * 3
        + [
            pltpu.VMEM((2, CORES, SIDE, slots + rows, half), BF16),
            pltpu.VMEM((2 * SIDE - 8 * slots // (slots + rows), slots + rows, half), BF16),
        ]
        + [pltpu.VMEM((2, slots + rows, half), BF16)] * 3
        + [
            pltpu.VMEM((SIDE,) + share, F32),
            pltpu.VMEM((count,) + share, F32),
            pltpu.VMEM(share, F32),
            pltpu.SemaphoreType.DMA((LAYER_COPIES,)),
            pltpu.SemaphoreType.DMA((LAYER_COPIES,)),
            pltpu.SemaphoreType.DMA((36,)),
        ],
        compiler_params=pltpu.CompilerParams(
            collective_id=0, has_side_effects=True, vmem_limit_bytes=VMEM_BYTES
        ),
        name="layer",
    )(tokens, out_grad, *tables, *dense, *expert)


def finish_kernel(out_grad, dense_sum, back, first_table, second_table, *rest):
    sources, input_grad, results, sems = rest[:6], rest[6], rest[7:13], rest[13]
    copies = []
    for source, result in zip(sources, results):
        pieces = 1 if source.shape[0] < 1024 else 7
        rows = source.shape[0] // pieces
        for i in range(pieces):
            at = pl.ds(i * rows, rows)
            copies.append(
                pltpu.make_async_copy(source.at[at], result.at[at], sems.at[len(copies)])
            )
            copies[-1].start()
    columns = back.shape[2]
    for k in range(4):
        cols = pl.ds(k * columns, columns)
        table = (first_table, second_table)[k % 2]
        picked = jnp.dot(table[...], back[k // 2], preferred_element_type=F32)
        input_grad[:, cols] = (
            out_grad[:, cols].astype(F32) + dense_sum[:, cols] + picked
        ).astype(BF16)
    for copy in copies:
        copy.wait()


def finish(out_grad, dense_sum, back, first_table, second_table, grads):
    return pl.pallas_call(
        finish_kernel,
        out_shape=[jax.ShapeDtypeStruct(out_grad.shape, BF16)]
        + [jax.ShapeDtypeStruct(grad.shape, BF16) for grad in grads],
        in_specs=[VMEM] * 5 + [ANY] * 6,
        out_specs=[VMEM] + [ANY] * 6,
        scratch_shapes=[pltpu.SemaphoreType.DMA((24,))],
        compiler_params=pltpu.CompilerParams(vmem_limit_bytes=60 << 20),
        name="finish",
    )(out_grad, dense_sum, back, first_table, second_table, *grads)


def local(
    tokens, out_grad, gate_weights, expert_ids, dense_gate, dense_up, dense_down,
    expert_gate, expert_up, expert_down,
):
    tok_dev, width = tokens.shape
    nodes = SIDE * SIDE
    capacity = 4 * tok_dev // nodes
    block = 2 * capacity
    flat_ids = expert_ids.reshape(-1)
    pair = jnp.arange(2 * tok_dev, dtype=jnp.int32)
    earlier = (flat_ids[:, None] == flat_ids[None, :]) & (pair[None, :] < pair[:, None])
    slot_index = jnp.sum(earlier.astype(jnp.int32), axis=1)
    position = (flat_ids * block + slot_index).reshape(tok_dev, 2)
    row = jnp.arange(nodes * block, dtype=jnp.int32)[None, :, None]
    first_hit = (row == position[:, None, :]).astype(F32)
    second_hit = (row == position[:, None, :] + capacity).astype(F32)
    first_table = jnp.sum(first_hit, axis=2).astype(BF16)
    second_table = jnp.sum(second_hit, axis=2).astype(BF16)
    weights = gate_weights.astype(F32)[:, None, :]
    first_weight = jnp.sum(first_hit * weights, axis=2).astype(BF16)
    second_weight = jnp.sum(second_hit * weights, axis=2).astype(BF16)
    back, dense_sum, back_shares, *sums = layer(
        tokens, out_grad, (first_table, second_table, first_weight, second_weight),
        (dense_gate, dense_up, dense_down), (expert_gate[0], expert_up[0], expert_down[0]),
    )
    input_grad, *weight_grads = finish(
        out_grad, dense_sum, back, first_table, second_table, sums
    )
    node, tensor = lax.axis_index("node"), lax.axis_index("tensor")
    start = lax.rem(tensor, CORES) * (nodes * capacity) + node * capacity
    mine = lax.dynamic_slice(back_shares, (0, 0, start), (nodes, 1, capacity)).reshape(1, 1, nodes, capacity)
    expert = jnp.arange(nodes, dtype=jnp.int32)[None, None, :, None]
    slot = jnp.arange(capacity, dtype=jnp.int32)[None, None, None, :]
    chosen = (expert == expert_ids[:, :, None, None]) & (
        slot == slot_index.reshape(tok_dev, 2)[:, :, None, None]
    )
    weighted = jnp.sum(jnp.where(chosen, mine, 0.0), axis=(2, 3))
    gate_weight_grad = weighted / gate_weights.astype(F32)
    return (
        input_grad,
        gate_weight_grad,
        *weight_grads[:3],
        *(value[None] for value in weight_grads[3:]),
    )


def solution(mesh):
    rows = P(("node", "tensor"), None)
    dense = P(None, "tensor")
    expert = P("node", None, "tensor")
    summed = P("node", "tensor")
    return jax.shard_map(
        local,
        mesh=mesh,
        in_specs=(rows,) * 4 + (dense,) * 3 + (expert,) * 3,
        out_specs=(rows, rows) + (summed,) * 3 + (expert,) * 3,
        check_vma=False,
    )
```

time: 182 us -> 422 us (2.32)
  Pallas kernels: 168 us -> 416 us
  local copies, waits for them, and re-layouts: 9.53 us -> 1.98 us
    pallas_call x1, Pallas kernels: 4.58 us -> 269 us  [finish(): pl.pallas_call(finish_kernel, out_shape=[jax.ShapeDtypeStruct(out_grad.sh...]
    pallas_call x2 -> x1, Pallas kernels: 163 us -> 147 us  [layer(): pl.pallas_call(layer_kernel, out_shape=[shape((2, 2 * slots, half // 2),...]
    unnamed x27 -> x5, local copies, waits for them, and re-layouts: 8.32 us -> 0.77 us
where the time goes in v2:
time: 422 us
  Pallas kernels  416 us (99%)
    pallas_call x1, Pallas kernels, finish(): pl.pallas_call(finish_kernel, out_shape=[jax.ShapeDtypeStruct(out_grad.sh...  269 us
    pallas_call x1, Pallas kernels, layer(): pl.pallas_call(layer_kernel, out_shape=[shape((2, 2 * slots, half // 2),...  147 us

profile of v2, /device:TPU:0, one launch (start us, length us, event | category | flops | bytes accessed | tf_op | source)
XLA Modules:
  0.0 421.6 jit_solution(318990769145242645)
XLA Ops:
  0.6 0.8 copy.40
  1.4 0.1 eq.78
  1.5 0.2 convert_reduce_fusion.2
  1.7 0.1 reduce_sum.57
  1.8 0.1 copy.41
  1.9 0.7 broadcast_add_fusion
  2.6 0.7 convert_element_type.30
  3.2 0.7 select_reduce_fusion.1
  3.9 146.8 %layer.1 = (bf16[2,256,896]{2,1,0:T(8,128)(2,1)}, f32[32,3584]{1,0:T(8,128)}, f32[16,8,256]{2,1,0:T(8,128)}, bf16[224,384]{1,0:T(8,128)(2,1)}, bf16[224,384]{1,0...) custom-call(bf16[32,3584]{1,0:T(8,128)(2,1)} %tok.1, ...), custom_call_target="tpu_custom_call" | custom-call | tf_op jit(solution)/shard_map/layer/pallas_call | solution.py:628
  150.8 0.0 copy-start
  150.8 0.0 copy-start.1
  150.8 269.2 %finish.1 = (bf16[32,3584]{1,0:T(8,128)(2,1)}, bf16[224,384]{1,0:T(8,128)(2,1)}, bf16[224,384]{1,0:T(8,128)(2,1)}, bf16[224,384]{1,0:T(8,128)(2,1)}, bf16[3584,3...) custom-call(bf16[32,3584]{1,0:T(8,128)(2,1)} %out_grad.1, ...), custom_call_target="tpu_custom_call" | custom-call | tf_op jit(solution)/shard_map/finish/pallas_call | solution.py:699
  420.0 0.9 constant_dynamic-slice_fusion
  420.9 0.0 copy-done
  421.0 0.1 select_reduce_fusion
  421.1 0.0 copy-done.1
  421.1 0.6 convert_divide_fusion
  (2 shorter events, 0.0 us)
Async XLA Ops:
  150.8 270.2 %copy-start = (s32[32,2]{0,1:T(2,128)S(1)}, s32[32,2]{0,1:T(2,128)}, u32[]{:S(2)}) copy-start(s32[32,2]{0,1:T(2,128)} %param.13) | copy-start | bytes 772
  150.8 270.3 %copy-start.1 = (bf16[32,2]{0,1:T(2,128)(2,1)S(1)}, bf16[32,2]{0,1:T(2,128)(2,1)}, u32[]{:S(2)}) copy-start(bf16[32,2]{0,1:T(2,128)(2,1)} %param.12) | copy-start | bytes 388

commit v3 on v2

--- a/solution.py
+++ b/solution.py
@@ -134,6 +134,12 @@
         self.to_left[0].wait_recv()
         self.pass_on(0, self.right_at, "right")
 
+    def take(self, half):
+        self.to_right[half].wait_recv()
+        self.pass_on(half, self.left_at, "left")
+        self.to_left[half].wait_recv()
+        self.pass_on(half, self.right_at, "right")
+
     def relay_far(self):
         self.relay_right.wait_recv()
         self.pass_on(0, self.far_at, "far")
@@ -189,7 +195,7 @@
 TILE = 512
 HALF_TILE = 256
 VMEM_BYTES = 63 << 20
-LAYER_COPIES = 2 * 14 + 2 * 15 + 24 + 8 + 12 + 7 + 15 + 2 * 15
+LAYER_COPIES = 14 + 12 + 1 + 3 * 15 + 24 + 8 + 12 + 7 + 15 + 2 * 15
 
 
 def silu_parts(pre_gate):
@@ -317,12 +323,12 @@
 
 
 def layer_kernel(
-    tok, grad, first_table, second_table, first_weight, second_weight,
-    dense_gate, dense_up, dense_down, expert_gate, expert_up, expert_down,
+    tok, grad, tables, dense_gate, dense_up, dense_down, expert_gate, expert_up, expert_down,
     back, dense_sum, back_shares, out_gate, out_up, out_down, gate_grad, up_grad, down_grad,
     tok_all, grad_all, rows_x, rows_dy, exchange, w_both, w_down, dense_parts, dense_hidden,
     parts, hidden, grads, relayed, from_left, from_right,
-    terms, core_rest, y_relayed, y_left, y_right, shares, share_in, share_sum,
+    terms, core_rest, y_relayed, y_left, y_right, far_tables,
+    shares, share_in, share_sum,
     send_sems, recv_sems, local_sems,
 ):
     x, z, y, core = place()
@@ -366,10 +372,11 @@
     dense.start(0)
     dense.start(1)
     exchanged = []
-    for h, (source, left, right) in enumerate(
-        ((tok, first_table, second_table), (grad, first_weight, second_weight))
-    ):
+    far = (node, dense.far_at)
+    tables_sent = net.start(tables, far_tables, far)
+    for h, source in enumerate((tok, grad)):
         out, into = outgoing[h], landed[h]
+        left, right = tables.at[2 * h], tables.at[2 * h + 1]
         for first in range(0, columns, 2 * HALF_TILE):
             width = min(2 * HALF_TILE, columns - first)
             value = lax.dot_general(
@@ -390,7 +397,7 @@
     col = lax.broadcasted_iota(jnp.int32, (slots, 2 * slots), 1)
     half = block // 2
     origin = lax.div(row, half) * block + lax.rem(row, half)
-    tables = [(col == origin + k * half).astype(F32).astype(BF16) for k in range(2)]
+    join_tables = [(col == origin + k * half).astype(F32).astype(BF16) for k in range(2)]
     row = lax.broadcasted_iota(jnp.int32, (2 * slots, slots), 0)
     col = lax.broadcasted_iota(jnp.int32, (2 * slots, slots), 1)
     origin = lax.div(row, block) * half + lax.rem(row, block)
@@ -411,7 +418,7 @@
             cols = pl.ds(first, width)
             for k in range(2):
                 own[:, pl.ds(k * columns + first, width)] = jnp.dot(
-                    tables[k], into[:, cols], preferred_element_type=F32
+                    join_tables[k], into[:, cols], preferred_element_type=F32
                 ).astype(BF16)
 
     dense.relay()
@@ -419,6 +426,47 @@
     join(0)
     routed.start(0)
     dense.relay_far()
+    tables_sent.wait_recv()
+    quarter = columns // 2
+    far_rows = pl.ds(pl.multiple_of(dense.far_at * local_rows, local_rows), local_rows)
+    for h, source in enumerate((tok_all, grad_all)):
+        for k in range(2):
+            value = lax.dot_general(
+                far_tables[2 * h], source[far_rows, pl.ds(2 * k * quarter, quarter)], TN,
+                preferred_element_type=F32,
+            ) + lax.dot_general(
+                far_tables[2 * h + 1], source[far_rows, pl.ds((2 * k + 1) * quarter, quarter)], TN,
+                preferred_element_type=F32,
+            )
+            grads[:, :, pl.ds((2 * h + k) * block, block), pl.ds(0, quarter)] = value.astype(
+                BF16
+            ).reshape(SIDE, SIDE, block, quarter)
+
+    def far_block(ref, index, first):
+        at = (lax.div(index, SIDE), lax.rem(index, SIDE), pl.ds(first, 4 * block), pl.ds(0, quarter))
+        return ref.at[at]
+
+    far_copies = [
+        net.start(far_block(grads, peer[0], 0), far_block(grads, node, 4 * block), peer, False)
+        for peer in peers
+    ]
+    far_kept = fetch(far_block(grads, node, 0), far_block(grads, node, 4 * block))
+
+    def join_far():
+        for copy in far_copies:
+            copy.wait()
+        far_kept.wait()
+        for h in range(2):
+            into = routed.chunk(h, routed.far_at)
+            for k in range(2):
+                value = grads[:, :, pl.ds((4 + 2 * h + k) * block, block), pl.ds(0, quarter)]
+                value = value.reshape(SIDE * SIDE * block, quarter)
+                for q in range(2):
+                    into[:, pl.ds((2 * k + q) * quarter, quarter)] = jnp.dot(
+                        join_tables[q], value, preferred_element_type=F32
+                    ).astype(BF16)
+            routed.pass_on(h, routed.far_at, "far")
+
     join(1)
     routed.start(1)
 
@@ -443,6 +491,67 @@
 
         input_term(dense_parts, w_both, c * columns, columns, keep_dense)
     weights = fetch_weights(expert_gate, expert_up, expert_down)
+    for copy in weights:
+        copy.wait()
+
+    pair = CORES * slots
+    crossed = {}
+
+    def from_core(step, c):
+        index, rows = 2 * step + c, slots + local_rows
+        fit = exchange.shape[0] // rows
+        if index < fit:
+            return exchange.at[pl.ds(index * rows, rows)]
+        return core_rest.at[index - fit]
+
+    def expert_rows(step, at):
+        rows = pl.ds(pl.multiple_of(at * pair, pair), pair)
+        product = unit_grads(
+            rows_x.at[rows], rows_dy.at[rows], w_both, w_down, parts.at[rows], hidden.at[rows]
+        )
+        shares[at] = lane_sums(product)
+        for c in range(2):
+
+            def keep_routed(cols, value, c=c):
+                for k in range(CORES):
+                    terms[c, side(k), at, pl.ds(0, slots), cols] = value[k * slots : (k + 1) * slots]
+
+            input_term(parts.at[rows], w_both, c * columns, columns, keep_routed)
+            crossed[step, c] = net.start(
+                terms.at[c, 1, at], from_core(step, c), routed.partner
+            )
+
+    def absorb(step, at, c):
+        crossed[step, c].wait_recv()
+        mine = terms.at[c, 0, at]
+        total(mine, [mine, from_core(step, c)])
+
+    def half_rows(ref, *lead):
+        half = ref.shape[-2] // 2
+        return lambda h: ref.at[(*lead, pl.ds(h * half, half))]
+
+    y_rings = [
+        RingSum(
+            net, y, routed.right, routed.left,
+            lambda position, h, c=c: half_rows(terms, c, 0, position)(h),
+            half_rows(y_relayed, c), half_rows(y_left, c), half_rows(y_right, c),
+        )
+        for c in range(2)
+    ]
+    routed.arrive("own")
+    expert_rows(0, y)
+    routed.take(0)
+    routed.take(1)
+    routed.arrive("left")
+    expert_rows(1, turn(y, 3))
+    routed.arrive("right")
+    expert_rows(2, turn(y, 1))
+    for c in range(2):
+        absorb(1, turn(y, 3), c)
+        y_rings[c].start_behind()
+        absorb(2, turn(y, 1), c)
+        y_rings[c].start_ahead()
+    join_far()
     band = depth // SIDE
     x_ring, z_ring = sums.rings
     for steps in (2, 1, 3, 0):
@@ -465,70 +574,6 @@
     z_ring.start_far()
     z_ring.start_ahead()
     z_ring.start_behind()
-    for copy in weights:
-        copy.wait()
-
-    pair = CORES * slots
-    crossed = {}
-
-    def from_core(step, c):
-        index, rows = 2 * step + c, slots + local_rows
-        fit = exchange.shape[0] // rows
-        if index < fit:
-            return exchange.at[pl.ds(index * rows, rows)]
-        return core_rest.at[index - fit]
-
-    def expert_rows(step, at):
-        rows = pl.ds(pl.multiple_of(at * pair, pair), pair)
-        product = unit_grads(
-            rows_x.at[rows], rows_dy.at[rows], w_both, w_down, parts.at[rows], hidden.at[rows]
-        )
-        shares[at] = lane_sums(product)
-        for c in range(2):
-
-            def keep_routed(cols, value, c=c):
-                for k in range(CORES):
-                    terms[c, side(k), at, pl.ds(0, slots), cols] = value[k * slots : (k + 1) * slots]
-
-            input_term(parts.at[rows], w_both, c * columns, columns, keep_routed)
-            crossed[step, c] = net.start(
-                terms.at[c, 1, at], from_core(step, c), routed.partner
-            )
-
-    def absorb(step, at, c):
-        crossed[step, c].wait_recv()
-        mine = terms.at[c, 0, at]
-        total(mine, [mine, from_core(step, c)])
-
-    def half_rows(ref, *lead):
-        half = ref.shape[-2] // 2
-        return lambda h: ref.at[(*lead, pl.ds(h * half, half))]
-
-    y_rings = [
-        RingSum(
-            net, y, routed.right, routed.left,
-            lambda position, h, c=c: half_rows(terms, c, 0, position)(h),
-            half_rows(y_relayed, c), half_rows(y_left, c), half_rows(y_right, c),
-        )
-        for c in range(2)
-    ]
-    routed.arrive("own")
-    expert_rows(0, y)
-    routed.relay()
-    routed.relay_rest()
-    sums.middle()
-    routed.arrive("left")
-    expert_rows(1, turn(y, 3))
-    routed.arrive("right")
-    sums.second()
-    expert_rows(2, turn(y, 1))
-    for c in range(2):
-        absorb(1, turn(y, 3), c)
-        absorb(2, turn(y, 1), c)
-    routed.relay_far()
-    for ring in y_rings:
-        ring.start_ahead()
-        ring.start_behind()
     routed.arrive("far")
     expert_rows(3, turn(y, 2))
     for c in range(2):
@@ -537,7 +582,6 @@
     share_copies = [
         net.start(shares.at[lax.div(mate[1], CORES)], share_in.at[tensor], mate) for mate in mates
     ]
-    sums.middle()
     for c in range(2):
         absorb(0, y, c)
 
@@ -569,12 +613,11 @@
     y_rings[0].middle()
     weight_tiles(3, 5)
     y_rings[1].middle()
-    sums.finish((out_gate, out_up, out_down))
+    sums.middle()
     count_tiles = depth // TILE
     short = columns // 2
     for c in range(2):
-        if c == 0:
-            weight_tiles(5, 6)
+        weight_tiles(5 + c, 6 + c)
         y_rings[c].finish()
         own, left, right = terms.at[c, 0, y], y_left.at[c], y_right.at[c]
         landed_rows = [ref.at[pl.ds(0, slots)] for ref in (own, left, right)]
@@ -605,7 +648,11 @@
             dense_sum.at[:, pl.ds(c * columns, columns)],
             [ref.at[pl.ds(slots, local_rows)] for ref in (own, left, right)],
         )
-    weight_tiles(6, count_tiles)
+        if c == 0:
+            sums.second()
+    sums.middle()
+    weight_tiles(7, count_tiles)
+    sums.finish((out_gate, out_up, out_down))
     for copy in returned:
         copy.wait_recv()
     for copy in written:
@@ -618,7 +665,7 @@
     hid = dense[0].shape[1]
     count = SIDE * CORES
     nodes = SIDE * SIDE
-    slots = tables[0].shape[1] // 2
+    slots = tables.shape[2] // 2
     node_rows, slot_rows = count * rows, count * slots
     own = depth // nodes
     half = depth // 2
@@ -634,7 +681,7 @@
         ]
         + [shape((own, hid), BF16)] * 3
         + [shape((depth, hid), BF16)] * 3,
-        in_specs=[VMEM] * 6 + [ANY] * 6,
+        in_specs=[VMEM] * 3 + [ANY] * 6,
         out_specs=[ANY] + [VMEM] * 5 + [ANY] * 3,
         scratch_shapes=[
             pltpu.VMEM((node_rows, depth), BF16),
@@ -657,6 +704,7 @@
         ]
         + [pltpu.VMEM((2, slots + rows, half), BF16)] * 3
         + [
+            pltpu.VMEM(tables.shape, BF16),
             pltpu.VMEM((SIDE,) + share, F32),
             pltpu.VMEM((count,) + share, F32),
             pltpu.VMEM(share, F32),
@@ -668,44 +716,48 @@
             collective_id=0, has_side_effects=True, vmem_limit_bytes=VMEM_BYTES
         ),
         name="layer",
-    )(tokens, out_grad, *tables, *dense, *expert)
-
-
-def finish_kernel(out_grad, dense_sum, back, first_table, second_table, *rest):
-    sources, input_grad, results, sems = rest[:6], rest[6], rest[7:13], rest[13]
-    copies = []
-    for source, result in zip(sources, results):
+    )(tokens, out_grad, tables, *dense, *expert)
+
+
+def finish_kernel(out_grad, dense_sum, back, tables, *rest):
+    sources, input_grad, results = rest[:6], rest[6], rest[7:13]
+    buffers, in_sems, out_sems = rest[13:19], rest[19], rest[20]
+    loads, stores = [], []
+    for source, buffer, result in zip(sources, buffers, results):
         pieces = 1 if source.shape[0] < 1024 else 7
         rows = source.shape[0] // pieces
         for i in range(pieces):
             at = pl.ds(i * rows, rows)
-            copies.append(
-                pltpu.make_async_copy(source.at[at], result.at[at], sems.at[len(copies)])
-            )
-            copies[-1].start()
+            k = len(loads)
+            loads.append(pltpu.make_async_copy(source.at[at], buffer.at[at], in_sems.at[k]))
+            stores.append(pltpu.make_async_copy(buffer.at[at], result.at[at], out_sems.at[k]))
+            loads[k].start()
     columns = back.shape[2]
     for k in range(4):
         cols = pl.ds(k * columns, columns)
-        table = (first_table, second_table)[k % 2]
-        picked = jnp.dot(table[...], back[k // 2], preferred_element_type=F32)
+        picked = jnp.dot(tables[k % 2], back[k // 2], preferred_element_type=F32)
         input_grad[:, cols] = (
             out_grad[:, cols].astype(F32) + dense_sum[:, cols] + picked
         ).astype(BF16)
-    for copy in copies:
-        copy.wait()
-
-
-def finish(out_grad, dense_sum, back, first_table, second_table, grads):
+        for load, store in list(zip(loads, stores))[k::4]:
+            load.wait()
+            store.start()
+    for store in stores:
+        store.wait()
+
+
+def finish(out_grad, dense_sum, back, tables, grads):
     return pl.pallas_call(
         finish_kernel,
         out_shape=[jax.ShapeDtypeStruct(out_grad.shape, BF16)]
         + [jax.ShapeDtypeStruct(grad.shape, BF16) for grad in grads],
-        in_specs=[VMEM] * 5 + [ANY] * 6,
+        in_specs=[VMEM] * 4 + [ANY] * 6,
         out_specs=[VMEM] + [ANY] * 6,
-        scratch_shapes=[pltpu.SemaphoreType.DMA((24,))],
+        scratch_shapes=[pltpu.VMEM(grad.shape, BF16) for grad in grads]
+        + [pltpu.SemaphoreType.DMA((24,))] * 2,
         compiler_params=pltpu.CompilerParams(vmem_limit_bytes=60 << 20),
         name="finish",
-    )(out_grad, dense_sum, back, first_table, second_table, *grads)
+    )(out_grad, dense_sum, back, tables, *grads)
 
 
 def local(
@@ -722,20 +774,16 @@
     slot_index = jnp.sum(earlier.astype(jnp.int32), axis=1)
     position = (flat_ids * block + slot_index).reshape(tok_dev, 2)
     row = jnp.arange(nodes * block, dtype=jnp.int32)[None, :, None]
-    first_hit = (row == position[:, None, :]).astype(F32)
-    second_hit = (row == position[:, None, :] + capacity).astype(F32)
-    first_table = jnp.sum(first_hit, axis=2).astype(BF16)
-    second_table = jnp.sum(second_hit, axis=2).astype(BF16)
-    weights = gate_weights.astype(F32)[:, None, :]
-    first_weight = jnp.sum(first_hit * weights, axis=2).astype(BF16)
-    second_weight = jnp.sum(second_hit * weights, axis=2).astype(BF16)
+    offset = jnp.array([0, capacity, 0, capacity], jnp.int32)[:, None, None, None]
+    hit = (row == position[:, None, :] + offset).astype(F32)
+    weights = jnp.stack([jnp.ones_like(gate_weights), gate_weights]).astype(F32)
+    weights = jnp.repeat(weights, 2, axis=0)[:, :, None, :]
+    tables = jnp.sum(hit * weights, axis=3).astype(BF16)
     back, dense_sum, back_shares, *sums = layer(
-        tokens, out_grad, (first_table, second_table, first_weight, second_weight),
+        tokens, out_grad, tables,
         (dense_gate, dense_up, dense_down), (expert_gate[0], expert_up[0], expert_down[0]),
     )
-    input_grad, *weight_grads = finish(
-        out_grad, dense_sum, back, first_table, second_table, sums
-    )
+    input_grad, *weight_grads = finish(out_grad, dense_sum, back, tables, sums)
     node, tensor = lax.axis_index("node"), lax.axis_index("tensor")
     start = lax.rem(tensor, CORES) * (nodes * capacity) + node * capacity
     mine = lax.dynamic_slice(back_shares, (0, 0, start), (nodes, 1, capacity)).reshape(1, 1, nodes, capacity)

time: 422 us -> 172 us (0.41)
  Pallas kernels: 416 us -> 164 us
    pallas_call x1, Pallas kernels: 269 us -> 9.1 us  [finish(): pl.pallas_call(finish_kernel, out_shape=[jax.ShapeDtypeStruct(out_grad.sh...]
    pallas_call x1, Pallas kernels: 147 us -> 155 us  [layer(): pl.pallas_call(layer_kernel, out_shape=[shape((2, 2 * slots, half // 2),...]
where the time goes in v3:
time: 172 us; the launch traced here: 171 us
  Pallas kernels  164 us (95%)
  other arithmetic  3.72 us (2%)
  local copies, waits for them, and re-layouts  1.99 us (1%)
    pallas_call x1, Pallas kernels, layer(): pl.pallas_call(layer_kernel, out_shape=[shape((2, 2 * slots, half // 2),...  155 us
    pallas_call x1, Pallas kernels, finish(): pl.pallas_call(finish_kernel, out_shape=[jax.ShapeDtypeStruct(out_grad.sh...  9.1 us

profile of v3, /device:TPU:0, one launch (start us, length us, event | category | flops | bytes accessed | tf_op | source)
XLA Modules:
  0.0 170.7 jit_solution(11908127195877340426)
XLA Ops:
  0.6 0.8 copy.40
  1.4 0.1 eq.65
  1.5 0.2 convert_reduce_fusion
  1.7 0.1 reduce_sum.30
  1.8 0.1 copy.41
  1.9 0.7 multiply_add_fusion
  2.6 0.7 broadcast_add_fusion
  3.3 0.7 pad_convert_fusion
  4.0 0.8 select_reduce_fusion.tables
  4.7 155.2 %layer.1 = (bf16[2,256,896]{2,1,0:T(8,128)(2,1)}, f32[32,3584]{1,0:T(8,128)}, f32[16,8,256]{2,1,0:T(8,128)}, bf16[224,384]{1,0:T(8,128)(2,1)}, bf16[224,384]{1,0...) custom-call(bf16[32,3584]{1,0:T(8,128)(2,1)} %tok.1, ...), custom_call_target="tpu_custom_call" | custom-call | tf_op jit(solution)/shard_map/layer/pallas_call | solution.py:675
  159.9 0.0 copy-start
  160.0 0.0 copy-start.1
  160.0 9.1 %finish.1 = (bf16[32,3584]{1,0:T(8,128)(2,1)}, bf16[224,384]{1,0:T(8,128)(2,1)}, bf16[224,384]{1,0:T(8,128)(2,1)}, bf16[224,384]{1,0:T(8,128)(2,1)}, bf16[3584,3...) custom-call(bf16[32,3584]{1,0:T(8,128)(2,1)} %out_grad.1, ...), custom_call_target="tpu_custom_call" | custom-call | tf_op jit(solution)/shard_map/finish/pallas_call | solution.py:750
  169.1 0.9 constant_dynamic-slice_fusion
  170.0 0.0 copy-done
  170.1 0.1 select_reduce_fusion.1
  170.2 0.0 copy-done.1
  170.2 0.6 convert_divide_fusion
  (3 shorter events, 0.0 us)
Async XLA Ops:
  159.9 10.1 %copy-start = (s32[32,2]{0,1:T(2,128)S(1)}, s32[32,2]{0,1:T(2,128)}, u32[]{:S(2)}) copy-start(s32[32,2]{0,1:T(2,128)} %param.14) | copy-start | bytes 772
  160.0 10.2 %copy-start.1 = (bf16[32,2]{0,1:T(2,128)(2,1)S(1)}, bf16[32,2]{0,1:T(2,128)(2,1)}, u32[]{:S(2)}) copy-start(bf16[32,2]{0,1:T(2,128)(2,1)} %param.13) | copy-start | bytes 388

commit v4 on v2

--- a/solution.py
+++ b/solution.py
@@ -134,6 +134,33 @@
         self.to_left[0].wait_recv()
         self.pass_on(0, self.right_at, "right")
 
+    def take(self, half):
+        self.to_right[half].wait_recv()
+        self.pass_on(half, self.left_at, "left")
+        self.to_left[half].wait_recv()
+        self.pass_on(half, self.right_at, "right")
+
+    def part_of(self, half, at, k):
+        rows = self.rows // 2
+        first = pl.multiple_of(at * self.rows + k * rows, rows)
+        return self.whole[half].at[pl.ds(first, rows)]
+
+    def take_and_relay(self, half):
+        send = self.net.start
+        self.to_right[half].wait_recv()
+        ref = self.part_of(half, self.left_at, 0)
+        self.relay_right = send(ref, ref, self.right)
+        self.pass_on(half, self.left_at, "left")
+        self.to_left[half].wait_recv()
+        ref = self.part_of(half, self.right_at, 1)
+        self.relay_left = send(ref, ref, self.left)
+        self.pass_on(half, self.right_at, "right")
+
+    def take_far(self, half):
+        self.relay_right.wait_recv()
+        self.relay_left.wait_recv()
+        self.pass_on(half, self.far_at, "far")
+
     def relay_far(self):
         self.relay_right.wait_recv()
         self.pass_on(0, self.far_at, "far")
@@ -188,8 +215,9 @@
 TN = (((0,), (0,)), ((), ()))
 TILE = 512
 HALF_TILE = 256
+TERM_TILE = 256
 VMEM_BYTES = 63 << 20
-LAYER_COPIES = 2 * 14 + 2 * 15 + 24 + 8 + 12 + 7 + 15 + 2 * 15
+LAYER_COPIES = 2 * 14 + 1 + 3 * 15 + 24 + 8 + 12 + 7 + 15 + 2 * 15
 
 
 def silu_parts(pre_gate):
@@ -210,16 +238,16 @@
     return hidden * hidden_grad
 
 
-def input_term(parts, w_both, first, columns, store):
+def input_term(parts, w_both, first, columns, store, tile=TERM_TILE):
     def body(i, carry):
-        at = pl.multiple_of(i * HALF_TILE, HALF_TILE)
+        at = pl.multiple_of(i * tile, tile)
         value = lax.dot_general(
-            parts[...], w_both[pl.ds(first + at, HALF_TILE)], NT, preferred_element_type=F32
+            parts[...], w_both[pl.ds(first + at, tile)], NT, preferred_element_type=F32
         )
-        store(pl.ds(at, HALF_TILE), value.astype(BF16))
+        store(pl.ds(at, tile), value.astype(BF16))
         return carry
 
-    lax.fori_loop(0, columns // HALF_TILE, body, 0)
+    lax.fori_loop(0, columns // tile, body, 0)
 
 
 def lane_sums(value):
@@ -229,6 +257,37 @@
     return lax.dot_general(ones, high, NT, preferred_element_type=F32) + lax.dot_general(
         ones, low, NT, preferred_element_type=F32
     )
+
+
+def routing(meta, slots, tokens, block):
+    experts = SIDE * SIDE
+    expert = lax.broadcasted_iota(jnp.int32, (experts, tokens), 0).astype(F32)
+    named = [(expert == meta[k : k + 1, :tokens]).astype(F32) for k in range(2)]
+    row = lax.broadcasted_iota(jnp.int32, (tokens, tokens), 0)
+    col = lax.broadcasted_iota(jnp.int32, (tokens, tokens), 1)
+    earlier = jnp.dot(
+        (named[0] + named[1]).astype(BF16),
+        (row < col).astype(F32).astype(BF16),
+        preferred_element_type=F32,
+    )
+    slot = [jnp.sum(earlier * hit, axis=0, keepdims=True) for hit in named]
+    weight = [meta[2 + k : 3 + k, :tokens] for k in range(2)]
+    return named, slot, weight
+
+
+def routing_tables(meta, slots, tokens, block):
+    unused, slot, weight = routing(meta, slots, tokens, block)
+    row = lax.broadcasted_iota(jnp.int32, (2 * slots, tokens), 0).astype(F32)
+    tables = []
+    for weighted in range(2):
+        for second in range(2):
+            table = jnp.zeros((2 * slots, tokens), F32)
+            for k in range(2):
+                position = meta[k : k + 1, :tokens] * block + slot[k] + second * (block // 2)
+                value = weight[k] if weighted else jnp.ones_like(weight[k])
+                table = table + jnp.where(row == position, value, 0.0)
+            tables.append(table.astype(BF16))
+    return tables
 
 
 class WeightSums:
@@ -317,12 +376,11 @@
 
 
 def layer_kernel(
-    tok, grad, first_table, second_table, first_weight, second_weight,
-    dense_gate, dense_up, dense_down, expert_gate, expert_up, expert_down,
+    tok, grad, meta, dense_gate, dense_up, dense_down, expert_gate, expert_up, expert_down,
     back, dense_sum, back_shares, out_gate, out_up, out_down, gate_grad, up_grad, down_grad,
-    tok_all, grad_all, rows_x, rows_dy, exchange, w_both, w_down, dense_parts, dense_hidden,
-    parts, hidden, grads, relayed, from_left, from_right,
-    terms, core_rest, y_relayed, y_left, y_right, shares, share_in, share_sum,
+    tok_all, grad_all, rows_x, rows_dy, exchange, w_both, w_down, parts, hidden, grads, relayed, from_left, from_right,
+    terms, core_rest, y_relayed, y_left, y_right, far_meta,
+    shares, share_in, share_sum,
     send_sems, recv_sems, local_sems,
 ):
     x, z, y, core = place()
@@ -339,6 +397,8 @@
     landed = [exchange.at[pl.ds((2 + h) * stack, stack)] for h in range(2)]
     block = stack // (SIDE * SIDE)
     slots = stack // 2
+    far_pair = pl.ds(pl.multiple_of(turn(y, 2) * stack, stack), stack)
+    dense_parts, dense_hidden = parts.at[far_pair], hidden.at[far_pair]
     started = []
 
     def fetch(src, dst):
@@ -366,17 +426,16 @@
     dense.start(0)
     dense.start(1)
     exchanged = []
-    for h, (source, left, right) in enumerate(
-        ((tok, first_table, second_table), (grad, first_weight, second_weight))
-    ):
+    meta_sent = net.start(meta, far_meta, (node, dense.far_at))
+    tables = routing_tables(meta[...], slots, local_rows, block)
+    for h, source in enumerate((tok, grad)):
         out, into = outgoing[h], landed[h]
+        left, right = tables[2 * h], tables[2 * h + 1]
         for first in range(0, columns, 2 * HALF_TILE):
             width = min(2 * HALF_TILE, columns - first)
-            value = lax.dot_general(
-                left[...], source[:, pl.ds(first, width)], TN, preferred_element_type=F32
-            ) + lax.dot_general(
-                right[...], source[:, pl.ds(columns + first, width)], TN, preferred_element_type=F32
-            )
+            value = jnp.dot(
+                left, source[:, pl.ds(first, width)], preferred_element_type=F32
+            ) + jnp.dot(right, source[:, pl.ds(columns + first, width)], preferred_element_type=F32)
             out[:, pl.ds(first, width)] = value.astype(BF16)
         exchanged.append(
             [net.start(rows_of(out, peer[0]), rows_of(into, node), peer, False) for peer in peers]
@@ -390,7 +449,7 @@
     col = lax.broadcasted_iota(jnp.int32, (slots, 2 * slots), 1)
     half = block // 2
     origin = lax.div(row, half) * block + lax.rem(row, half)
-    tables = [(col == origin + k * half).astype(F32).astype(BF16) for k in range(2)]
+    join_tables = [(col == origin + k * half).astype(F32).astype(BF16) for k in range(2)]
     row = lax.broadcasted_iota(jnp.int32, (2 * slots, slots), 0)
     col = lax.broadcasted_iota(jnp.int32, (2 * slots, slots), 1)
     origin = lax.div(row, block) * half + lax.rem(row, block)
@@ -411,7 +470,7 @@
             cols = pl.ds(first, width)
             for k in range(2):
                 own[:, pl.ds(k * columns + first, width)] = jnp.dot(
-                    tables[k], into[:, cols], preferred_element_type=F32
+                    join_tables[k], into[:, cols], preferred_element_type=F32
                 ).astype(BF16)
 
     dense.relay()
@@ -419,6 +478,54 @@
     join(0)
     routed.start(0)
     dense.relay_far()
+    meta_sent.wait_recv()
+    tables = routing_tables(far_meta[...], slots, local_rows, block)[:2]
+    far_rows = pl.ds(pl.multiple_of(dense.far_at * local_rows, local_rows), local_rows)
+    far_y = turn(y, 2)
+    for first in range(0, columns, 2 * HALF_TILE):
+        width = min(2 * HALF_TILE, columns - first)
+        value = (
+            jnp.dot(tables[0], tok_all[far_rows, pl.ds(first, width)], preferred_element_type=F32)
+            + jnp.dot(
+                tables[1],
+                tok_all[far_rows, pl.ds(columns + first, width)],
+                preferred_element_type=F32,
+            )
+        ).astype(BF16)
+        for c in range(2):
+            terms[c, 1, far_y, pl.ds(0, slots), pl.ds(first, width)] = value[
+                c * slots : (c + 1) * slots
+            ]
+    each = SIDE * SIDE // 2
+
+    def far_leaving(index):
+        rows = pl.ds(pl.multiple_of(lax.rem(index, each) * block, block), block)
+        return terms.at[lax.div(index, each), 1, far_y, rows]
+
+    def far_landing(index):
+        rows = pl.ds(pl.multiple_of(lax.rem(index, each) * block, block), block)
+        return core_rest.at[lax.div(index, each), rows]
+
+    far_copies = [
+        net.start(far_leaving(peer[0]), far_landing(node), peer, False) for peer in peers
+    ]
+    far_kept = fetch(far_leaving(node), far_landing(node))
+
+    def join_far():
+        for copy in far_copies:
+            copy.wait()
+        far_kept.wait()
+        for c in range(2):
+            rows = pl.ds(pl.multiple_of(routed.far_at * slots + c * (slots // 2), slots // 2), slots // 2)
+            for first in range(0, columns, 2 * HALF_TILE):
+                width = min(2 * HALF_TILE, columns - first)
+                value = core_rest[c, pl.ds(0, slots), pl.ds(first, width)]
+                for k in range(2):
+                    rows_x[rows, pl.ds(k * columns + first, width)] = jnp.dot(
+                        join_tables[k][: slots // 2, :slots], value, preferred_element_type=F32
+                    ).astype(BF16)
+        routed.pass_on(0, routed.far_at, "far")
+
     join(1)
     routed.start(1)
 
@@ -514,21 +621,21 @@
     ]
     routed.arrive("own")
     expert_rows(0, y)
-    routed.relay()
-    routed.relay_rest()
+    routed.take(0)
+    join_far()
     sums.middle()
+    routed.take_and_relay(1)
     routed.arrive("left")
     expert_rows(1, turn(y, 3))
+    for c in range(2):
+        absorb(1, turn(y, 3), c)
+        y_rings[c].start_behind()
     routed.arrive("right")
-    sums.second()
     expert_rows(2, turn(y, 1))
     for c in range(2):
-        absorb(1, turn(y, 3), c)
         absorb(2, turn(y, 1), c)
-    routed.relay_far()
-    for ring in y_rings:
-        ring.start_ahead()
-        ring.start_behind()
+        y_rings[c].start_ahead()
+    routed.take_far(1)
     routed.arrive("far")
     expert_rows(3, turn(y, 2))
     for c in range(2):
@@ -537,7 +644,6 @@
     share_copies = [
         net.start(shares.at[lax.div(mate[1], CORES)], share_in.at[tensor], mate) for mate in mates
     ]
-    sums.middle()
     for c in range(2):
         absorb(0, y, c)
 
@@ -565,16 +671,16 @@
     share_sum[...] = value
     back_shares[node] = value
     returned = [net.start(share_sum, back_shares.at[node], peer) for peer in peers]
-    weight_tiles(2, 3)
+    sums.second()
     y_rings[0].middle()
-    weight_tiles(3, 5)
+    weight_tiles(2, 4)
     y_rings[1].middle()
-    sums.finish((out_gate, out_up, out_down))
+    weight_tiles(4, 5)
+    sums.middle()
     count_tiles = depth // TILE
     short = columns // 2
     for c in range(2):
-        if c == 0:
-            weight_tiles(5, 6)
+        weight_tiles(5 + c, 6 + c)
         y_rings[c].finish()
         own, left, right = terms.at[c, 0, y], y_left.at[c], y_right.at[c]
         landed_rows = [ref.at[pl.ds(0, slots)] for ref in (own, left, right)]
@@ -605,7 +711,8 @@
             dense_sum.at[:, pl.ds(c * columns, columns)],
             [ref.at[pl.ds(slots, local_rows)] for ref in (own, left, right)],
         )
-    weight_tiles(6, count_tiles)
+    weight_tiles(7, count_tiles)
+    sums.finish((out_gate, out_up, out_down))
     for copy in returned:
         copy.wait_recv()
     for copy in written:
@@ -613,12 +720,11 @@
     net.drain()
 
 
-def layer(tokens, out_grad, tables, dense, expert):
+def layer(tokens, out_grad, meta, slots, dense, expert):
     rows, depth = tokens.shape
     hid = dense[0].shape[1]
     count = SIDE * CORES
     nodes = SIDE * SIDE
-    slots = tables[0].shape[1] // 2
     node_rows, slot_rows = count * rows, count * slots
     own = depth // nodes
     half = depth // 2
@@ -634,7 +740,7 @@
         ]
         + [shape((own, hid), BF16)] * 3
         + [shape((depth, hid), BF16)] * 3,
-        in_specs=[VMEM] * 6 + [ANY] * 6,
+        in_specs=[VMEM] * 3 + [ANY] * 6,
         out_specs=[ANY] + [VMEM] * 5 + [ANY] * 3,
         scratch_shapes=[
             pltpu.VMEM((node_rows, depth), BF16),
@@ -644,8 +750,6 @@
             pltpu.VMEM((8 * slots, half), BF16),
             pltpu.VMEM((depth, 2 * hid), BF16),
             pltpu.VMEM((depth, hid), BF16),
-            pltpu.VMEM((node_rows, 2 * hid), BF16),
-            pltpu.VMEM((node_rows, hid), BF16),
             pltpu.VMEM((slot_rows, 2 * hid), BF16),
             pltpu.VMEM((slot_rows, hid), BF16),
             pltpu.VMEM((SIDE, SIDE, own, 3 * hid), BF16),
@@ -657,6 +761,7 @@
         ]
         + [pltpu.VMEM((2, slots + rows, half), BF16)] * 3
         + [
+            pltpu.VMEM(meta.shape, F32),
             pltpu.VMEM((SIDE,) + share, F32),
             pltpu.VMEM((count,) + share, F32),
             pltpu.VMEM(share, F32),
@@ -668,90 +773,91 @@
             collective_id=0, has_side_effects=True, vmem_limit_bytes=VMEM_BYTES
         ),
         name="layer",
-    )(tokens, out_grad, *tables, *dense, *expert)
-
-
-def finish_kernel(out_grad, dense_sum, back, first_table, second_table, *rest):
-    sources, input_grad, results, sems = rest[:6], rest[6], rest[7:13], rest[13]
-    copies = []
-    for source, result in zip(sources, results):
+    )(tokens, out_grad, meta, *dense, *expert)
+
+
+def finish_kernel(out_grad, dense_sum, back, meta, back_shares, *rest):
+    sources, input_grad, share, results = rest[:6], rest[6], rest[7], rest[8:14]
+    buffers, in_sems, out_sems = rest[14:20], rest[20], rest[21]
+    loads, stores = [], []
+    for source, buffer, result in zip(sources, buffers, results):
         pieces = 1 if source.shape[0] < 1024 else 7
         rows = source.shape[0] // pieces
         for i in range(pieces):
             at = pl.ds(i * rows, rows)
-            copies.append(
-                pltpu.make_async_copy(source.at[at], result.at[at], sems.at[len(copies)])
-            )
-            copies[-1].start()
-    columns = back.shape[2]
+            k = len(loads)
+            loads.append(pltpu.make_async_copy(source.at[at], buffer.at[at], in_sems.at[k]))
+            stores.append(pltpu.make_async_copy(buffer.at[at], result.at[at], out_sems.at[k]))
+            loads[k].start()
+    nodes, tokens = SIDE * SIDE, out_grad.shape[0]
+    slots, columns = back.shape[1] // 2, back.shape[2]
+    block = 2 * slots // nodes
+    named, slot, weight = routing(meta[...], slots, tokens, block)
+    first = lax.axis_index("node") * (block // 2)
+    first = first + lax.rem(lax.axis_index("tensor"), CORES) * slots
+    lane = lax.broadcasted_iota(jnp.int32, (block // 2, CORES * slots), 1)
+    wanted = lax.broadcasted_iota(jnp.int32, (block // 2, CORES * slots), 0) + first
+    wanted = (lane == wanted).astype(F32).astype(BF16)
+
+    def split(value):
+        high = value.astype(BF16)
+        return high, (value - high.astype(F32)).astype(BF16)
+
+    mine = sum(
+        lax.dot_general(wanted, part, NT, preferred_element_type=F32)
+        for part in split(back_shares[:, 0, :])
+    )
+    index = lax.broadcasted_iota(jnp.int32, (block // 2, tokens), 0).astype(F32)
+    for k in range(2):
+        value = sum(
+            jnp.dot(part, named[k].astype(BF16), preferred_element_type=F32) for part in split(mine)
+        )
+        value = jnp.sum(jnp.where(index == slot[k], value, 0.0), axis=0, keepdims=True)
+        share[pl.ds(k, 1), :] = value / weight[k]
+    for load, store in zip(loads, stores):
+        load.wait()
+        store.start()
+    tables = routing_tables(meta[...], slots, tokens, block)
     for k in range(4):
         cols = pl.ds(k * columns, columns)
-        table = (first_table, second_table)[k % 2]
-        picked = jnp.dot(table[...], back[k // 2], preferred_element_type=F32)
+        picked = lax.dot_general(tables[k % 2], back[k // 2], TN, preferred_element_type=F32)
         input_grad[:, cols] = (
             out_grad[:, cols].astype(F32) + dense_sum[:, cols] + picked
         ).astype(BF16)
-    for copy in copies:
-        copy.wait()
-
-
-def finish(out_grad, dense_sum, back, first_table, second_table, grads):
+    for store in stores:
+        store.wait()
+
+
+def finish(out_grad, dense_sum, back, meta, back_shares, grads):
     return pl.pallas_call(
         finish_kernel,
-        out_shape=[jax.ShapeDtypeStruct(out_grad.shape, BF16)]
+        out_shape=[
+            jax.ShapeDtypeStruct(out_grad.shape, BF16),
+            jax.ShapeDtypeStruct((2, out_grad.shape[0]), F32),
+        ]
         + [jax.ShapeDtypeStruct(grad.shape, BF16) for grad in grads],
         in_specs=[VMEM] * 5 + [ANY] * 6,
-        out_specs=[VMEM] + [ANY] * 6,
-        scratch_shapes=[pltpu.SemaphoreType.DMA((24,))],
+        out_specs=[VMEM] * 2 + [ANY] * 6,
+        scratch_shapes=[pltpu.VMEM(grad.shape, BF16) for grad in grads]
+        + [pltpu.SemaphoreType.DMA((24,))] * 2,
         compiler_params=pltpu.CompilerParams(vmem_limit_bytes=60 << 20),
         name="finish",
-    )(out_grad, dense_sum, back, first_table, second_table, *grads)
+    )(out_grad, dense_sum, back, meta, back_shares, *grads)
 
 
 def local(
     tokens, out_grad, gate_weights, expert_ids, dense_gate, dense_up, dense_down,
     expert_gate, expert_up, expert_down,
 ):
-    tok_dev, width = tokens.shape
-    nodes = SIDE * SIDE
-    capacity = 4 * tok_dev // nodes
-    block = 2 * capacity
-    flat_ids = expert_ids.reshape(-1)
-    pair = jnp.arange(2 * tok_dev, dtype=jnp.int32)
-    earlier = (flat_ids[:, None] == flat_ids[None, :]) & (pair[None, :] < pair[:, None])
-    slot_index = jnp.sum(earlier.astype(jnp.int32), axis=1)
-    position = (flat_ids * block + slot_index).reshape(tok_dev, 2)
-    row = jnp.arange(nodes * block, dtype=jnp.int32)[None, :, None]
-    first_hit = (row == position[:, None, :]).astype(F32)
-    second_hit = (row == position[:, None, :] + capacity).astype(F32)
-    first_table = jnp.sum(first_hit, axis=2).astype(BF16)
-    second_table = jnp.sum(second_hit, axis=2).astype(BF16)
-    weights = gate_weights.astype(F32)[:, None, :]
-    first_weight = jnp.sum(first_hit * weights, axis=2).astype(BF16)
-    second_weight = jnp.sum(second_hit * weights, axis=2).astype(BF16)
+    slots = 4 * tokens.shape[0]
+    meta = jnp.concatenate([expert_ids.T.astype(F32), gate_weights.T.astype(F32)], axis=0)
+    meta = jnp.pad(meta, ((0, 4), (0, 128 - meta.shape[1])))
     back, dense_sum, back_shares, *sums = layer(
-        tokens, out_grad, (first_table, second_table, first_weight, second_weight),
-        (dense_gate, dense_up, dense_down), (expert_gate[0], expert_up[0], expert_down[0]),
+        tokens, out_grad, meta, slots, (dense_gate, dense_up, dense_down),
+        (expert_gate[0], expert_up[0], expert_down[0]),
     )
-    input_grad, *weight_grads = finish(
-        out_grad, dense_sum, back, first_table, second_table, sums
-    )
-    node, tensor = lax.axis_index("node"), lax.axis_index("tensor")
-    start = lax.rem(tensor, CORES) * (nodes * capacity) + node * capacity
-    mine = lax.dynamic_slice(back_shares, (0, 0, start), (nodes, 1, capacity)).reshape(1, 1, nodes, capacity)
-    expert = jnp.arange(nodes, dtype=jnp.int32)[None, None, :, None]
-    slot = jnp.arange(capacity, dtype=jnp.int32)[None, None, None, :]
-    chosen = (expert == expert_ids[:, :, None, None]) & (
-        slot == slot_index.reshape(tok_dev, 2)[:, :, None, None]
-    )
-    weighted = jnp.sum(jnp.where(chosen, mine, 0.0), axis=(2, 3))
-    gate_weight_grad = weighted / gate_weights.astype(F32)
-    return (
-        input_grad,
-        gate_weight_grad,
-        *weight_grads[:3],
-        *(value[None] for value in weight_grads[3:]),
-    )
+    input_grad, share, *sums = finish(out_grad, dense_sum, back, meta, back_shares, sums)
+    return (input_grad, share.T, *sums[:3], *(value[None] for value in sums[3:]))
 
 
 def solution(mesh):

time: 422 us -> 153 us (0.36)
  Pallas kernels: 416 us -> 150 us
    pallas_call x1, Pallas kernels: 269 us -> 9.43 us  [finish(): pl.pallas_call(finish_kernel, out_shape=[jax.ShapeDtypeStruct(out_grad.sh...]
    pallas_call x1, Pallas kernels: 147 us -> 141 us  [layer(): pl.pallas_call(layer_kernel, out_shape=[shape((2, 2 * slots, half // 2),...]
where the time goes in v4:
time: 153 us
  Pallas kernels  150 us (98%)
  other arithmetic  1.94 us (1%)
    pallas_call x1, Pallas kernels, layer(): pl.pallas_call(layer_kernel, out_shape=[shape((2, 2 * slots, half // 2),...  141 us
    pallas_call x1, Pallas kernels, finish(): pl.pallas_call(finish_kernel, out_shape=[jax.ShapeDtypeStruct(out_grad.sh...  9.43 us

profile of v4, /device:TPU:0, one launch (start us, length us, event | category | flops | bytes accessed | tf_op | source)
XLA Modules:
  0.0 153.2 jit_solution(5507494990673679668)
XLA Ops:
  0.6 0.7 convert_bitcast_fusion
  1.3 0.7 convert_bitcast_fusion.1
  2.0 0.6 select_maximum_fusion.meta
  2.6 141.0 %layer.1 = (bf16[2,256,896]{2,1,0:T(8,128)(2,1)}, f32[32,3584]{1,0:T(8,128)}, f32[16,8,256]{2,1,0:T(8,128)}, bf16[224,384]{1,0:T(8,128)(2,1)}, bf16[224,384]{1,0...) custom-call(bf16[32,3584]{1,0:T(8,128)(2,1)} %tok.1, ...), custom_call_target="tpu_custom_call" | custom-call | tf_op jit(solution)/shard_map/layer/pallas_call | solution.py:734
  143.5 9.4 %finish.1 = (bf16[32,3584]{1,0:T(8,128)(2,1)}, f32[2,32]{1,0:T(2,128)}, bf16[224,384]{1,0:T(8,128)(2,1)}, bf16[224,384]{1,0:T(8,128)(2,1)}, bf16[224,384]{1,0:T(...) custom-call(bf16[32,3584]{1,0:T(8,128)(2,1)} %out_grad.1, ...), custom_call_target="tpu_custom_call" | custom-call | tf_op jit(solution)/shard_map/finish/pallas_call | solution.py:832

commit v5 on v4

--- a/solution.py
+++ b/solution.py
@@ -102,24 +102,33 @@
         self.right = (node, self.right_at)
         self.left = (node, self.left_at)
         self.partner = (node, y * CORES + 1 - core)
+        self.sent = []
         self.crossed, self.to_right, self.to_left = {}, {}, {}
+
+    def send(self, src, dst, peer):
+        self.sent.append(self.net.start(src, dst, peer, False))
+        return self.sent[-1]
+
+    def flush(self):
+        for copy in self.sent:
+            copy.wait_send()
 
     def chunk(self, half, at):
         return self.whole[half].at[pl.ds(pl.multiple_of(at * self.rows, self.rows), self.rows)]
 
     def pass_on(self, half, at, name):
         ref = self.chunk(half, at)
-        self.crossed[name, half] = self.net.start(ref, ref, self.partner)
+        self.crossed[name, half] = self.send(ref, ref, self.partner)
 
     def start(self, half):
-        send = self.net.start
+        send = self.send
         mine, own = self.chunk(half, self.me), self.own[half]
         self.to_right[half] = send(own, mine, self.right)
         self.to_left[half] = send(own, mine, self.left)
         self.crossed["own", half] = send(own, mine, self.partner)
 
     def relay(self):
-        send = self.net.start
+        send = self.send
         left_at, right_at = self.left_at, self.right_at
         self.to_right[0].wait_recv()
         self.relay_right = send(self.chunk(0, left_at), self.chunk(0, left_at), self.right)
@@ -146,7 +155,7 @@
         return self.whole[half].at[pl.ds(first, rows)]
 
     def take_and_relay(self, half):
-        send = self.net.start
+        send = self.send
         self.to_right[half].wait_recv()
         ref = self.part_of(half, self.left_at, 0)
         self.relay_right = send(ref, ref, self.right)
@@ -167,8 +176,8 @@
         self.relay_left.wait_recv()
         self.pass_on(1, self.far_at, "far")
 
-    def arrive(self, name):
-        for half in range(2):
+    def arrive(self, name, halves=(0, 1)):
+        for half in halves:
             self.crossed[name, half].wait_recv()
 
 
@@ -225,9 +234,10 @@
     return (pre_gate * sigma, sigma * (1.0 + pre_gate * (1.0 - sigma)))
 
 
-def unit_grads(rows_x, rows_dy, w_both, w_down, parts, hidden_out):
+def unit_grads(rows_x, rows_dy, w_both, w_down, parts, hidden_out, pre=None):
     hid = w_down.shape[1]
-    pre = jnp.dot(rows_x[...], w_both[...], preferred_element_type=F32)
+    if pre is None:
+        pre = jnp.dot(rows_x[...], w_both[...], preferred_element_type=F32)
     hidden_grad = jnp.dot(rows_dy[...], w_down[...], preferred_element_type=F32)
     pre_up = pre[:, hid:]
     activated, derivative = silu_parts(pre[:, :hid])
@@ -288,6 +298,13 @@
                 table = table + jnp.where(row == position, value, 0.0)
             tables.append(table.astype(BF16))
     return tables
+
+
+def fill(meta, ids, weights):
+    tokens = ids.shape[1]
+    meta[...] = jnp.zeros_like(meta)
+    meta[pl.ds(0, 2), pl.ds(0, tokens)] = ids[...].astype(F32)
+    meta[pl.ds(2, 2), pl.ds(0, tokens)] = weights[...].astype(F32)
 
 
 class WeightSums:
@@ -376,10 +393,10 @@
 
 
 def layer_kernel(
-    tok, grad, meta, dense_gate, dense_up, dense_down, expert_gate, expert_up, expert_down,
+    tok, grad, ids, gates, dense_gate, dense_up, dense_down, expert_gate, expert_up, expert_down,
     back, dense_sum, back_shares, out_gate, out_up, out_down, gate_grad, up_grad, down_grad,
     tok_all, grad_all, rows_x, rows_dy, exchange, w_both, w_down, parts, hidden, grads, relayed, from_left, from_right,
-    terms, core_rest, y_relayed, y_left, y_right, far_meta,
+    terms, core_rest, y_relayed, y_left, y_right, meta, far_meta,
     shares, share_in, share_sum,
     send_sems, recv_sems, local_sems,
 ):
@@ -426,6 +443,7 @@
     dense.start(0)
     dense.start(1)
     exchanged = []
+    fill(meta, ids, gates)
     meta_sent = net.start(meta, far_meta, (node, dense.far_at))
     tables = routing_tables(meta[...], slots, local_rows, block)
     for h, source in enumerate((tok, grad)):
@@ -585,10 +603,26 @@
             return exchange.at[pl.ds(index * rows, rows)]
         return core_rest.at[index - fit]
 
+    def early_place(step):
+        ref, first = ((tok_all, 0), (tok_all, 4 * hid), (grad_all, 0))[step - 1]
+        return [ref.at[:, pl.ds(first + k * 2 * hid, 2 * hid)] for k in range(2)]
+
+    def early_rows(step, at):
+        rows = pl.ds(pl.multiple_of(at * pair, pair), pair)
+        pre = jnp.dot(rows_x[rows], w_both[...], preferred_element_type=F32)
+        high, low = early_place(step)
+        rounded = pre.astype(BF16)
+        high[...] = rounded
+        low[...] = (pre - rounded.astype(F32)).astype(BF16)
+
     def expert_rows(step, at):
         rows = pl.ds(pl.multiple_of(at * pair, pair), pair)
+        pre = None
+        if step:
+            high, low = early_place(step)
+            pre = high[...].astype(F32) + low[...].astype(F32)
         product = unit_grads(
-            rows_x.at[rows], rows_dy.at[rows], w_both, w_down, parts.at[rows], hidden.at[rows]
+            rows_x.at[rows], rows_dy.at[rows], w_both, w_down, parts.at[rows], hidden.at[rows], pre
         )
         shares[at] = lane_sums(product)
         for c in range(2):
@@ -623,24 +657,29 @@
     expert_rows(0, y)
     routed.take(0)
     join_far()
+    dense.flush()
+    for step, (name, at) in enumerate((("left", 3), ("right", 1), ("far", 2))):
+        routed.arrive(name, (0,))
+        early_rows(step + 1, turn(y, at))
+    routed.take_and_relay(1)
     sums.middle()
-    routed.take_and_relay(1)
-    routed.arrive("left")
+    routed.arrive("left", (1,))
     expert_rows(1, turn(y, 3))
     for c in range(2):
         absorb(1, turn(y, 3), c)
         y_rings[c].start_behind()
-    routed.arrive("right")
+    routed.arrive("right", (1,))
     expert_rows(2, turn(y, 1))
     for c in range(2):
         absorb(2, turn(y, 1), c)
         y_rings[c].start_ahead()
     routed.take_far(1)
-    routed.arrive("far")
+    routed.arrive("far", (1,))
     expert_rows(3, turn(y, 2))
     for c in range(2):
         absorb(3, turn(y, 2), c)
         y_rings[c].start_far()
+    sums.second()
     share_copies = [
         net.start(shares.at[lax.div(mate[1], CORES)], share_in.at[tensor], mate) for mate in mates
     ]
@@ -671,7 +710,6 @@
     share_sum[...] = value
     back_shares[node] = value
     returned = [net.start(share_sum, back_shares.at[node], peer) for peer in peers]
-    sums.second()
     y_rings[0].middle()
     weight_tiles(2, 4)
     y_rings[1].middle()
@@ -717,10 +755,11 @@
         copy.wait_recv()
     for copy in written:
         copy.wait()
+    routed.flush()
     net.drain()
 
 
-def layer(tokens, out_grad, meta, slots, dense, expert):
+def layer(tokens, out_grad, ids, gates, slots, dense, expert):
     rows, depth = tokens.shape
     hid = dense[0].shape[1]
     count = SIDE * CORES
@@ -740,7 +779,7 @@
         ]
         + [shape((own, hid), BF16)] * 3
         + [shape((depth, hid), BF16)] * 3,
-        in_specs=[VMEM] * 3 + [ANY] * 6,
+        in_specs=[VMEM] * 4 + [ANY] * 6,
         out_specs=[ANY] + [VMEM] * 5 + [ANY] * 3,
         scratch_shapes=[
             pltpu.VMEM((node_rows, depth), BF16),
@@ -761,7 +800,8 @@
         ]
         + [pltpu.VMEM((2, slots + rows, half), BF16)] * 3
         + [
-            pltpu.VMEM(meta.shape, F32),
+            pltpu.VMEM((8, 128), F32),
+            pltpu.VMEM((8, 128), F32),
             pltpu.VMEM((SIDE,) + share, F32),
             pltpu.VMEM((count,) + share, F32),
             pltpu.VMEM(share, F32),
@@ -773,12 +813,12 @@
             collective_id=0, has_side_effects=True, vmem_limit_bytes=VMEM_BYTES
         ),
         name="layer",
-    )(tokens, out_grad, meta, *dense, *expert)
-
-
-def finish_kernel(out_grad, dense_sum, back, meta, back_shares, *rest):
+    )(tokens, out_grad, ids, gates, *dense, *expert)
+
+
+def finish_kernel(out_grad, dense_sum, back, ids, gates, back_shares, *rest):
     sources, input_grad, share, results = rest[:6], rest[6], rest[7], rest[8:14]
-    buffers, in_sems, out_sems = rest[14:20], rest[20], rest[21]
+    buffers, in_sems, out_sems, meta = rest[14:20], rest[20], rest[21], rest[22]
     loads, stores = [], []
     for source, buffer, result in zip(sources, buffers, results):
         pieces = 1 if source.shape[0] < 1024 else 7
@@ -792,6 +832,7 @@
     nodes, tokens = SIDE * SIDE, out_grad.shape[0]
     slots, columns = back.shape[1] // 2, back.shape[2]
     block = 2 * slots // nodes
+    fill(meta, ids, gates)
     named, slot, weight = routing(meta[...], slots, tokens, block)
     first = lax.axis_index("node") * (block // 2)
     first = first + lax.rem(lax.axis_index("tensor"), CORES) * slots
@@ -828,7 +869,7 @@
         store.wait()
 
 
-def finish(out_grad, dense_sum, back, meta, back_shares, grads):
+def finish(out_grad, dense_sum, back, ids, gates, back_shares, grads):
     return pl.pallas_call(
         finish_kernel,
         out_shape=[
@@ -836,13 +877,14 @@
             jax.ShapeDtypeStruct((2, out_grad.shape[0]), F32),
         ]
         + [jax.ShapeDtypeStruct(grad.shape, BF16) for grad in grads],
-        in_specs=[VMEM] * 5 + [ANY] * 6,
+        in_specs=[VMEM] * 6 + [ANY] * 6,
         out_specs=[VMEM] * 2 + [ANY] * 6,
         scratch_shapes=[pltpu.VMEM(grad.shape, BF16) for grad in grads]
-        + [pltpu.SemaphoreType.DMA((24,))] * 2,
+        + [pltpu.SemaphoreType.DMA((24,))] * 2
+        + [pltpu.VMEM((8, 128), F32)],
         compiler_params=pltpu.CompilerParams(vmem_limit_bytes=60 << 20),
         name="finish",
-    )(out_grad, dense_sum, back, meta, back_shares, *grads)
+    )(out_grad, dense_sum, back, ids, gates, back_shares, *grads)
 
 
 def local(
@@ -850,13 +892,12 @@
     expert_gate, expert_up, expert_down,
 ):
     slots = 4 * tokens.shape[0]
-    meta = jnp.concatenate([expert_ids.T.astype(F32), gate_weights.T.astype(F32)], axis=0)
-    meta = jnp.pad(meta, ((0, 4), (0, 128 - meta.shape[1])))
+    ids, gates = expert_ids.T, gate_weights.T
     back, dense_sum, back_shares, *sums = layer(
-        tokens, out_grad, meta, slots, (dense_gate, dense_up, dense_down),
+        tokens, out_grad, ids, gates, slots, (dense_gate, dense_up, dense_down),
         (expert_gate[0], expert_up[0], expert_down[0]),
     )
-    input_grad, share, *sums = finish(out_grad, dense_sum, back, meta, back_shares, sums)
+    input_grad, share, *sums = finish(out_grad, dense_sum, back, ids, gates, back_shares, sums)
     return (input_grad, share.T, *sums[:3], *(value[None] for value in sums[3:]))
 
 

time: 153 us -> 148 us (0.967)
  Pallas kernels: 150 us -> 147 us
  other arithmetic: 1.94 us -> 0 us
    pallas_call x1, Pallas kernels: 141 us -> 137 us  [layer(): pl.pallas_call(layer_kernel, out_shape=[shape((2, 2 * slots, half // 2),...]
where the time goes in v5:
time: 148 us; the launch traced here: 147 us
  Pallas kernels  147 us (99%)
    pallas_call x1, Pallas kernels, layer(): pl.pallas_call(layer_kernel, out_shape=[shape((2, 2 * slots, half // 2),...  137 us
    pallas_call x1, Pallas kernels, finish(): pl.pallas_call(finish_kernel, out_shape=[jax.ShapeDtypeStruct(out_grad.sh...  9.46 us

profile of v5, /device:TPU:0, one launch (start us, length us, event | category | flops | bytes accessed | tf_op | source)
XLA Modules:
  0.0 147.4 jit_solution(1366137177453758983)
XLA Ops:
  0.6 137.1 %layer.1 = (bf16[2,256,896]{2,1,0:T(8,128)(2,1)}, f32[32,3584]{1,0:T(8,128)}, f32[16,8,256]{2,1,0:T(8,128)}, bf16[224,384]{1,0:T(8,128)(2,1)}, bf16[224,384]{1,0...) custom-call(bf16[32,3584]{1,0:T(8,128)(2,1)} %tok.1, ...), custom_call_target="tpu_custom_call" | custom-call | tf_op jit(solution)/shard_map/layer/pallas_call | solution.py:773
  137.7 9.5 %finish.1 = (bf16[32,3584]{1,0:T(8,128)(2,1)}, f32[2,32]{1,0:T(2,128)}, bf16[224,384]{1,0:T(8,128)(2,1)}, bf16[224,384]{1,0:T(8,128)(2,1)}, bf16[224,384]{1,0:T(...) custom-call(bf16[32,3584]{1,0:T(8,128)(2,1)} %out_grad.1, ...), custom_call_target="tpu_custom_call" | custom-call | tf_op jit(solution)/shard_map/finish/pallas_call | solution.py:873

commit v6 on v5

--- a/solution.py
+++ b/solution.py
@@ -832,6 +832,9 @@
     nodes, tokens = SIDE * SIDE, out_grad.shape[0]
     slots, columns = back.shape[1] // 2, back.shape[2]
     block = 2 * slots // nodes
+    for load, store in zip(loads, stores):
+        load.wait()
+        store.start()
     fill(meta, ids, gates)
     named, slot, weight = routing(meta[...], slots, tokens, block)
     first = lax.axis_index("node") * (block // 2)
@@ -855,9 +858,6 @@
         )
         value = jnp.sum(jnp.where(index == slot[k], value, 0.0), axis=0, keepdims=True)
         share[pl.ds(k, 1), :] = value / weight[k]
-    for load, store in zip(loads, stores):
-        load.wait()
-        store.start()
     tables = routing_tables(meta[...], slots, tokens, block)
     for k in range(4):
         cols = pl.ds(k * columns, columns)

time: 148 us -> 148 us (level)
  no operation moved by 1% of the time
where the time goes in v6:
time: 148 us; the launch traced here: 147 us
  Pallas kernels  147 us (99%)
    pallas_call x1, Pallas kernels, layer(): pl.pallas_call(layer_kernel, out_shape=[shape((2, 2 * slots, half // 2),...  137 us
    pallas_call x1, Pallas kernels, finish(): pl.pallas_call(finish_kernel, out_shape=[jax.ShapeDtypeStruct(out_grad.sh...  9.45 us

profile of v6, /device:TPU:0, one launch (start us, length us, event | category | flops | bytes accessed | tf_op | source)
XLA Modules:
  0.0 147.4 jit_solution(16743636712873452159)
XLA Ops:
  0.6 137.1 %layer.1 = (bf16[2,256,896]{2,1,0:T(8,128)(2,1)}, f32[32,3584]{1,0:T(8,128)}, f32[16,8,256]{2,1,0:T(8,128)}, bf16[224,384]{1,0:T(8,128)(2,1)}, bf16[224,384]{1,0...) custom-call(bf16[32,3584]{1,0:T(8,128)(2,1)} %tok.1, ...), custom_call_target="tpu_custom_call" | custom-call | tf_op jit(solution)/shard_map/layer/pallas_call | solution.py:773
  137.7 9.4 %finish.1 = (bf16[32,3584]{1,0:T(8,128)(2,1)}, f32[2,32]{1,0:T(2,128)}, bf16[224,384]{1,0:T(8,128)(2,1)}, bf16[224,384]{1,0:T(8,128)(2,1)}, bf16[224,384]{1,0:T(...) custom-call(bf16[32,3584]{1,0:T(8,128)(2,1)} %out_grad.1, ...), custom_call_target="tpu_custom_call" | custom-call | tf_op jit(solution)/shard_map/finish/pallas_call | solution.py:873
